TPU v7x, 128 devices: a whole 4x4x4 slice. The times are simulated.
128 devices in a mesh: video: 2 (over z_hi), tile: 32 (over y, x, core), section: 2 (over z_lo).
Axes of the slice: x: 4, y: 4, z: 4 (z_hi: 2, z_lo: 2; z = z_hi * 2 + z_lo), core: 2. Of those that a mesh axis runs over, the one named last changes fastest.
Arguments:
- latent: float32 [4, 32, 4, 16, 256], P('video', 'tile', 'section'), may hold values from -6 to 6
- resolution: int32 [4], replicated, may hold values from 0 to 1, as said below
- frame_counts: int32 [4], replicated, may hold values from 1 to 4, as said below
- tile_rows: int32 [4, 32], replicated, may hold values from 0 to 30, as said below
- tile_cols: int32 [4, 32], replicated, may hold values from 0 to 70, as said below
- decoder_list: int32 [4, 32], replicated, may hold values from -1 to 63, as said below
- w_in: bfloat16 [432, 384], replicated, may hold values from -0.3125 to 0.3125
- b_in: float32 [384], replicated, may hold values from -4 to 4
- gain_one: float32 [384], replicated, may hold values from 0.25 to 1.75
- w_one: bfloat16 [10368, 384], replicated, may hold values from -0.0625 to 0.0625
- b_one: float32 [384], replicated, may hold values from -4 to 4
- gain_two: float32 [384], replicated, may hold values from 0.25 to 1.75
- w_two: bfloat16 [10368, 384], replicated, may hold values from -0.0625 to 0.0625
- b_two: float32 [384], replicated, may hold values from -4 to 4
Outputs:
- decoded: bfloat16 [2, 32, 4, 100, 384], P('video', 'tile', 'section')
Inputs may be any that keep to these rules, and one draw needn't show every extreme that they name: `resolution`: 0 marks a 480p video, 1 a 720p one; both occur in every draw. `frame_counts`: frames at or after this count are not part of the video. `tile_rows`: a multiple of 10; a video of resolution r has its first (1 + r) * 8 slots live, placed on distinct tiles of a grid of 2 + 2 r rows and 8 columns of tiles; other slots hold 0. `tile_cols`: a multiple of 10, on the same grid; other slots hold 0. `decoder_list`: the decoder of a live slot, -1 for the other slots; no decoder is named twice.
All inputs are finite; a program needn't handle non-finite values.
Results may differ from a plain program's by a relative error of at most 0.0051.
Values may be sent and summed in bfloat16 or wider, within the bound.
No kernel may reach another device: no remote copies, remote signals or barrier semaphores. Data moves between devices by JAX's collectives and lax.ppermute only.
A program may use at most 128 MiB of HBM per device.

v0:
```python
import jax
import jax.numpy as jnp
from jax import lax
from jax.sharding import PartitionSpec as P


def from_behind(shard, axis, by):
    count = lax.axis_size(axis)
    pairs = [(i, i + by) for i in range(count) if 0 <= i + by < count]
    return lax.ppermute(shard, axis, pairs)


def inside_mask(tile_row, tile_col, resolved, margin, extent, interior, grid_cols):
    size = extent - 2 * margin
    offsets = jnp.arange(size, dtype=jnp.int32) + margin - 3
    grid_row = tile_row[:, None] + offsets[None, :]
    grid_col = tile_col[:, None] + offsets[None, :]
    high = (2 + 2 * resolved) * interior - 3
    row_ok = (grid_row >= 0) & (grid_row < high[:, None])
    col_ok = (grid_col >= 0) & (grid_col < grid_cols * interior - 4)
    return (row_ok[:, :, None] & col_ok[:, None, :]).astype(jnp.float32)[:, None, :, :, None]


def conv_valid(padded, weight, frames):
    batch_size = padded.shape[0]
    height = padded.shape[2] - 2
    width_out = padded.shape[3] - 2
    pieces = []
    for tap_time in range(3):
        for tap_row in range(3):
            for tap_col in range(3):
                pieces.append(
                    padded[
                        :,
                        tap_time : tap_time + frames,
                        tap_row : tap_row + height,
                        tap_col : tap_col + width_out,
                        :,
                    ]
                )
    columns = jnp.concatenate(pieces, axis=-1)
    flat = columns.reshape(batch_size * frames * height * width_out, columns.shape[-1])
    result = jnp.dot(flat, weight, preferred_element_type=jnp.float32)
    return result.reshape(batch_size, frames, height, width_out, weight.shape[1])


def normalize(values, gain):
    return values * lax.rsqrt(jnp.mean(values * values, axis=-1, keepdims=True) + 1e-06) * gain


def with_cache(field):
    earlier = from_behind(field, "section", 1)
    return jnp.concatenate([earlier, field], axis=1)


def decode_batch(latent_tile, tile_row, tile_col, resolved, counts, params):
    w_in, b_in, gain_one, w_one, b_one, gain_two, w_two, b_two = params
    batch_size = latent_tile.shape[0]
    frames = latent_tile.shape[1]
    extent = latent_tile.shape[2]
    channels_in = latent_tile.shape[3] // extent
    interior = extent - 6
    grid_cols = lax.axis_size("tile") // 4
    section_index = lax.axis_index("section")
    field = latent_tile.reshape(batch_size, frames, extent, extent, channels_in)
    first_frame = section_index * frames
    span = field.shape[1]
    known = (first_frame + jnp.arange(span, dtype=jnp.int32) >= 0).astype(jnp.float32)[
        None, :, None, None, None
    ]

    def prepare(values):
        return with_cache(values)

    mask_zero = inside_mask(tile_row, tile_col, resolved, 0, extent, interior, grid_cols)
    field = (field * mask_zero).astype(jnp.bfloat16)
    stem = conv_valid(prepare(field), w_in, span) + b_in
    mask_one = inside_mask(tile_row, tile_col, resolved, 1, extent, interior, grid_cols)
    act_one = (jax.nn.silu(normalize(stem, gain_one)) * mask_one * known).astype(jnp.bfloat16)
    middle = conv_valid(prepare(act_one), w_one, span) + b_one
    mask_two = inside_mask(tile_row, tile_col, resolved, 2, extent, interior, grid_cols)
    act_two = (jax.nn.silu(normalize(middle, gain_two)) * mask_two * known).astype(jnp.bfloat16)
    final = (
        conv_valid(prepare(act_two), w_two, span)
        + b_two
        + stem[:, :, 2 : 2 + interior, 2 : 2 + interior, :]
    )
    frame_index = section_index * frames + jnp.arange(frames, dtype=jnp.int32)
    valid = (frame_index[None, :] < counts[:, None]).astype(jnp.float32)[:, :, None, None, None]
    return (final * valid).reshape(batch_size, frames, interior * interior, final.shape[-1])


def local(
    latent,
    resolution,
    frame_counts,
    tile_rows,
    tile_cols,
    decoder_list,
    w_in,
    b_in,
    gain_one,
    w_one,
    b_one,
    gain_two,
    w_two,
    b_two,
):
    params = (w_in, b_in, gain_one, w_one, b_one, gain_two, w_two, b_two)
    per_group = latent.shape[0]
    tile_count = lax.axis_size("tile")
    video_count = lax.axis_size("video")
    peer_count = video_count * tile_count
    group_index = lax.axis_index("video")
    slot_index = lax.axis_index("tile")
    own_videos = group_index * per_group + jnp.arange(per_group, dtype=jnp.int32)
    video_iota = jnp.arange(decoder_list.shape[0], dtype=jnp.int32)
    slot_iota = jnp.arange(decoder_list.shape[1], dtype=jnp.int32)
    own_match = (video_iota[None, :, None] == own_videos[:, None, None]) & (
        slot_iota[None, None, :] == slot_index
    )
    video_match = video_iota[None, :] == own_videos[:, None]
    targets = jnp.sum(jnp.where(own_match, decoder_list[None], 0), axis=(1, 2))
    routing = (jnp.arange(peer_count, dtype=jnp.int32)[:, None] == targets[None, :]).astype(
        jnp.bfloat16
    )
    owned = latent[:, 0].astype(jnp.bfloat16)
    own_rows = jnp.sum(jnp.where(own_match, tile_rows[None], 0), axis=(1, 2))
    own_cols = jnp.sum(jnp.where(own_match, tile_cols[None], 0), axis=(1, 2))
    own_res = jnp.sum(jnp.where(video_match, resolution[None], 0), axis=1)
    own_counts = jnp.sum(jnp.where(video_match, frame_counts[None], 0), axis=1)
    decoded_own = decode_batch(owned, own_rows, own_cols, own_res, own_counts, params).astype(
        jnp.bfloat16
    )
    outgoing = jnp.einsum(
        "pj,jfnc->pfnc", routing, decoded_own, preferred_element_type=jnp.float32
    ).astype(jnp.bfloat16)
    arrived = lax.all_to_all(outgoing, ("video", "tile"), split_axis=0, concat_axis=0, tiled=True)
    decoded = jnp.sum(arrived, axis=0, dtype=jnp.float32).astype(jnp.bfloat16)
    return decoded[None, None]


def solution(mesh):
    return jax.shard_map(
        local,
        mesh=mesh,
        in_specs=(
            P("video", "tile", "section", None, None),
            P(),
            P(),
            P(),
            P(),
            P(),
            P(),
            P(),
            P(),
            P(),
            P(),
            P(),
            P(),
            P(),
        ),
        out_specs=P("video", "tile", "section", None, None),
        check_vma=False,
    )
```

profile of v0, /device:TPU:0, one launch (start us, length us, event | category | flops | bytes accessed | tf_op | source)
XLA Modules:
  0.0 280.5 jit_solution(17610625384884371281)
XLA Ops:
  0.0 0.9 convert_convert_fusion
  1.2 0.9 select_reduce_fusion
  2.1 1.0 fusion.57
  3.4 3.9 %collective-permute-start = (bf16[2,2,16,16,16]{4,3,2,1,0:T(8,128)(2,1)S(1)}, bf16[2,2,16,16,16]{4,3,2,1,0:T(8,128)(2,1)S(1)}, u32[]{:S(2)}, u32[]{:S(2)}) collective-permute-start(bf16[2,2,16,16,16]{4,3,2,1,0:T(8,128)(2,1)S(1)} %multiply_convert_fusion.2), channel_id=1, source_target_pairs={{0,1},{2,3},{4,5},{6,7},{8,9},{10,11},{12,13},{14,15},{16,17},{18,... | collective-permute-start | bytes 98312 | tf_op jit(solution)/shard_map/ppermute | solution.py:10
  7.3 0.2 fusion.64
  7.8 5.1 %collective-permute-done = bf16[2,2,16,16,16]{4,3,2,1,0:T(8,128)(2,1)S(1)} collective-permute-done((bf16[2,2,16,16,16]{4,3,2,1,0:T(8,128)(2,1)S(1)}, bf16[2,2,16,16,16]{4,3,2,1,0:T(8,128)(2,1)S(1)}, u32[]{:S(2)}, u32[]{:S(2)}) %collective-permute-start) | collective-permute-done | bytes 32800 | tf_op jit(solution)/shard_map/ppermute | solution.py:10
  12.9 1.4 fusion.65
  14.3 1.4 pad_maximum_fusion.2
  15.7 6.1 %concatenate.19 = bf16[2,2,14,14,432]{4,3,2,1,0:T(8,128)(2,1)} concatenate(bf16[2,2,14,14,16]{4,3,2,1,0:T(8,128)(2,1)} %get-tuple-element.36, bf16[2,2,14,14,16]{4,3,2,1,0:T(8,128)(2,1)} %get-tuple-element.35, bf16[2,2,14,14,16]{4,3,2,1,0:T(8,128)(2,1)} %get-tuple-element.34, bf16[2,2,14,14,16]{4,3,2,1,0:T(8,128)(2,1)} %get-tuple-element.33, ...), dimensions={4} | concatenate | bytes 1354752 | tf_op jit(solution)/shard_map/concatenate | solution.py:41
  21.8 1.9 multiply_reduce_fusion
  23.7 0.5 multiply_convert_fusion
  24.2 0.5 copy.72
  24.7 4.6 %collective-permute-start.1 = (bf16[2,2,14,14,384]{4,1,3,2,0:T(2,128)(2,1)S(1)}, bf16[2,2,14,14,384]{4,1,3,2,0:T(2,128)(2,1)S(1)}, u32[]{:S(2)}, u32[]{:S(2)}) collective-permute-start(bf16[2,2,14,14,384]{4,1,3,2,0:T(2,128)(2,1)S(1)} %copy.72), channel_id=1, source_target_pairs={{0,1},{2,3},{4,5},{6,7},{8,9},{10,11},{12,13},{14,15},{16,17},{18,... | collective-permute-start | bytes 1806344 | tf_op jit(solution)/shard_map/ppermute | solution.py:10
  29.5 11.6 %collective-permute-done.1 = bf16[2,2,14,14,384]{4,1,3,2,0:T(2,128)(2,1)S(1)} collective-permute-done((bf16[2,2,14,14,384]{4,1,3,2,0:T(2,128)(2,1)S(1)}, bf16[2,2,14,14,384]{4,1,3,2,0:T(2,128)(2,1)S(1)}, u32[]{:S(2)}, u32[]{:S(2)}) %collective-permute-start.1) | collective-permute-done | bytes 602144 | tf_op jit(solution)/shard_map/ppermute | solution.py:10
  41.2 0.2 slice_dynamic-update-slice_fusion.16
  41.5 0.2 slice_dynamic-update-slice_fusion.15
  41.8 0.2 slice_dynamic-update-slice_fusion.13
  42.1 0.2 slice_dynamic-update-slice_fusion.12
  42.4 0.2 slice_dynamic-update-slice_fusion.10
  42.7 0.2 slice_dynamic-update-slice_fusion.9
  43.1 0.2 fusion.17
  43.3 0.2 fusion.19
  43.7 0.2 fusion.23
  43.9 0.2 fusion.25
  44.3 0.2 fusion.13
  44.5 0.2 fusion.28
  44.8 0.2 slice_dynamic-update-slice_fusion.7
  45.1 0.2 slice_dynamic-update-slice_fusion.6
  45.4 0.2 slice_dynamic-update-slice_fusion.4
  45.7 0.2 slice_dynamic-update-slice_fusion.3
  46.0 0.2 slice_dynamic-update-slice_fusion.1
  46.3 0.2 slice_dynamic-update-slice_fusion
  46.6 8.5 %multiply_reduce_fusion.1 = (f32[2,2,12,12]{3,2,1,0:T(8,128)S(1)}, f32[2,2,12,12,384]{4,3,2,1,0:T(8,128)S(1)}) fusion(f32[384]{0:T(512)S(1)} %copy-done.5, bf16[2,2,12,12,10368]{4,3,2,1,0:T(8,128)(2,1)S(1)} %slice_dynamic-update-slice_fusion, bf16[10368,384]{1,0:T(8,128)(2,1)S(1)} %bitcast.44), kind=kOutput, calls=%fused_computation.43 | convolution fusion | flops 4587134464 | bytes 20795136 | tf_op jit(solution)/shard_map/dot_general | solution.py:43
  55.2 0.5 multiply_convert_fusion.1
  55.6 0.5 copy.83
  56.1 4.6 %collective-permute-start.2 = (bf16[2,2,12,12,384]{4,1,3,2,0:T(2,128)(2,1)S(1)}, bf16[2,2,12,12,384]{4,1,3,2,0:T(2,128)(2,1)S(1)}, u32[]{:S(2)}, u32[]{:S(2)}) collective-permute-start(bf16[2,2,12,12,384]{4,1,3,2,0:T(2,128)(2,1)S(1)} %copy.83), channel_id=1, source_target_pairs={{0,1},{2,3},{4,5},{6,7},{8,9},{10,11},{12,13},{14,15},{16,17},{18,... | collective-permute-start | bytes 1327112 | tf_op jit(solution)/shard_map/ppermute | solution.py:10
  60.8 7.3 %collective-permute-done.2 = bf16[2,2,12,12,384]{4,1,3,2,0:T(2,128)(2,1)S(1)} collective-permute-done((bf16[2,2,12,12,384]{4,1,3,2,0:T(2,128)(2,1)S(1)}, bf16[2,2,12,12,384]{4,1,3,2,0:T(2,128)(2,1)S(1)}, u32[]{:S(2)}, u32[]{:S(2)}) %collective-permute-start.2) | collective-permute-done | bytes 442400 | tf_op jit(solution)/shard_map/ppermute | solution.py:10
  70.2 0.2 fusion.40
  70.4 0.2 fusion.42
  70.7 0.2 fusion.30
  72.5 0.3 slice-done.3
  72.8 7.1 %fusion.11 = bf16[2,2,10,10,384]{4,3,2,1,0:T(8,128)(2,1)S(1)} fusion(f32[2,2,14,14,384]{4,3,2,1,0:T(8,128)S(1)} %get-tuple-element.44, f32[2,2]{1,0:T(2,128)S(1)} %compare_convert_fusion, f32[384]{0:T(512)S(1)} %copy-done.6, bf16[2,2,10,10,10368]{4,3,2,1,0:T(8,128)(2,1)S(1)} %slice_dynamic-update-slice_fusion.18, bf16[10368,384]{1,0:T(8,128)(2,1)S(1)} %bitcast.46), kind=kOutput, calls=%fused_computation.62 | convolution fusion | flops 3185664000 | bytes 17180176 | tf_op jit(solution)/shard_map/dot_general | solution.py:43
  79.9 0.3 copy.103
  80.2 3.2 %convolution_convert_fusion = bf16[64,2,100,384]{3,0,2,1:T(8,128)(2,1)S(1)} fusion(bf16[2,2,100,384]{3,0,2,1:T(2,128)(2,1)S(1)} %bitcast.41, s32[2]{0:T(128)S(1)} %get-tuple-element.5), kind=kOutput, calls=%fused_computation.4 | convolution fusion | flops 24576128 | bytes 10137608 | tf_op jit(solution)/shard_map/pj,jfnc->pfnc/dot_general | solution.py:135
  83.4 62.0 %copy.96 = bf16[64,2,100,384]{3,1,2,0:T(2,128)(2,1)S(1)} copy(bf16[64,2,100,384]{3,0,2,1:T(8,128)(2,1)S(1)} %convolution_convert_fusion) | data formatting | bytes 19660800 | tf_op jit(solution)/shard_map/convert_element_type | solution.py:137
  145.4 124.6 %all_to_all.5 = bf16[64,2,100,384]{3,1,2,0:T(2,128)(2,1)} all-to-all(bf16[64,2,100,384]{3,1,2,0:T(2,128)(2,1)S(1)} %copy.96), channel_id=1, replica_groups=mesh['video'=2,'tile'=32,'section'=2] {'video','tile'}, dimensions={0} | all-to-all | bytes 19660800 | tf_op jit(solution)/shard_map/all_to_all | solution.py:138
  270.0 9.6 %reduce_sum.82 = bf16[2,100,384]{2,0,1:T(2,128)(2,1)S(1)} reduce(bf16[64,2,100,384]{3,1,2,0:T(2,128)(2,1)} %all_to_all.5, bf16[]{:T(256)} %constant.58.clone.1), dimensions={0}, to_apply=%region_7.8 | reduce | flops 4838400 | bytes 9984002 | tf_op jit(solution)/shard_map/reduce_sum | solution.py:139
  279.7 0.8 copy.98
  (79 shorter events, 5.9 us)
Async XLA Ops:
  0.0 21.7 %copy-start = (bf16[432,384]{1,0:T(8,128)(2,1)S(1)}, bf16[432,384]{1,0:T(8,128)(2,1)}, u32[]{:S(2)}) copy-start(bf16[432,384]{1,0:T(8,128)(2,1)} %param.20) | copy-start | bytes 995332
  0.0 21.8 %copy-start.4 = (f32[384]{0:T(512)S(1)}, f32[384]{0:T(512)}, u32[]{:S(2)}) copy-start(f32[384]{0:T(512)} %param.21) | copy-start | bytes 4612
  0.0 23.7 %copy-start.3 = (f32[384]{0:T(512)S(1)}, f32[384]{0:T(512)}, u32[]{:S(2)}) copy-start(f32[384]{0:T(512)} %param.22) | copy-start | bytes 4612
  3.4 9.5 %collective-permute-start = (bf16[2,2,16,16,16]{4,3,2,1,0:T(8,128)(2,1)S(1)}, bf16[2,2,16,16,16]{4,3,2,1,0:T(8,128)(2,1)S(1)}, u32[]{:S(2)}, u32[]{:S(2)}) collective-permute-start(bf16[2,2,16,16,16]{4,3,2,1,0:T(8,128)(2,1)S(1)} %multiply_convert_fusion.2), channel_id=1, source_target_pairs={{0,1},{2,3},{4,5},{6,7},{8,9},{10,11},{12,13},{14,15},{16,17},{18,... | collective-permute-start | bytes 98312 | tf_op jit(solution)/shard_map/ppermute | solution.py:10
  24.7 16.4 %collective-permute-start.1 = (bf16[2,2,14,14,384]{4,1,3,2,0:T(2,128)(2,1)S(1)}, bf16[2,2,14,14,384]{4,1,3,2,0:T(2,128)(2,1)S(1)}, u32[]{:S(2)}, u32[]{:S(2)}) collective-permute-start(bf16[2,2,14,14,384]{4,1,3,2,0:T(2,128)(2,1)S(1)} %copy.72), channel_id=1, source_target_pairs={{0,1},{2,3},{4,5},{6,7},{8,9},{10,11},{12,13},{14,15},{16,17},{18,... | collective-permute-start | bytes 1806344 | tf_op jit(solution)/shard_map/ppermute | solution.py:10
  43.0 3.5 %slice-start = ((s8[7962624]{0:T(1024)(128)(4,1)}), s8[4194304]{0:T(1024)(128)(4,1)S(1)}, s32[]{:S(2)}) async-start(s8[7962624]{0:T(1024)(128)(4,1)} %bitcast.43), calls=%async_computation.1 | async-start | bytes 8388608
  43.1 3.4 %copy-start.5 = (f32[384]{0:T(512)S(1)}, f32[384]{0:T(512)}, u32[]{:S(2)}) copy-start(f32[384]{0:T(512)} %param.24) | copy-start | bytes 4612
  44.3 2.4 slice-start.1
  46.6 8.5 %copy-start.2 = (f32[384]{0:T(512)S(1)}, f32[384]{0:T(512)}, u32[]{:S(2)}) copy-start(f32[384]{0:T(512)} %param.25) | copy-start | bytes 4612
  56.1 12.0 %collective-permute-start.2 = (bf16[2,2,12,12,384]{4,1,3,2,0:T(2,128)(2,1)S(1)}, bf16[2,2,12,12,384]{4,1,3,2,0:T(2,128)(2,1)S(1)}, u32[]{:S(2)}, u32[]{:S(2)}) collective-permute-start(bf16[2,2,12,12,384]{4,1,3,2,0:T(2,128)(2,1)S(1)} %copy.83), channel_id=1, source_target_pairs={{0,1},{2,3},{4,5},{6,7},{8,9},{10,11},{12,13},{14,15},{16,17},{18,... | collective-permute-start | bytes 1327112 | tf_op jit(solution)/shard_map/ppermute | solution.py:10
  69.1 3.4 %slice-start.2 = ((s8[7962624]{0:T(1024)(128)(4,1)}), s8[4194304]{0:T(1024)(128)(4,1)S(1)}, s32[]{:S(2)}) async-start(s8[7962624]{0:T(1024)(128)(4,1)} %bitcast.45), calls=%async_computation.3 | async-start | bytes 8388608
  69.1 3.4 %copy-start.6 = (f32[384]{0:T(512)S(1)}, f32[384]{0:T(512)}, u32[]{:S(2)}) copy-start(f32[384]{0:T(512)} %param.27) | copy-start | bytes 4612
  70.6 2.2 slice-start.3
  83.4 197.1 %copy-start.1 = (bf16[432,384]{1,0:T(8,128)(2,1)S(1)}, bf16[432,384]{1,0:T(8,128)(2,1)}, u32[]{:S(2)}) copy-start(bf16[432,384]{1,0:T(8,128)(2,1)} %param.20) | copy-start | bytes 995332
where the time goes:
time: 282 us; the launch traced here: 281 us
  blocking collectives  125 us (44%)
  local copies, waits for them, and re-layouts  78.7 us (28%)
  waiting for transfers between devices  24 us (9%)
  matrix products  20.6 us (7%)
  other arithmetic  18.8 us (7%)
  starting transfers between devices  13.2 us (5%)
    all_to_all x1, blocking collectives, local(): lax.all_to_all(outgoing, ('video', 'tile'), split_axis=0, concat_axis=0,...  125 us
    convert_element_type x1, local copies, waits for them, and re-layouts, local(): outgoing = jnp.einsum('pj,jfnc->pfnc', routing, decoded_own, preferred_el...  62 us
    ppermute x3, waiting for transfers between devices, from_behind(): return lax.ppermute(shard, axis, pairs)  24 us
    dot_general x3, matrix products, conv_valid(): result = jnp.dot(flat, weight, preferred_element_type=jnp.float32)  17.4 us
    ppermute x3, starting transfers between devices, from_behind(): return lax.ppermute(shard, axis, pairs)  13.2 us
    reduce_sum x1, other arithmetic, local(): decoded = jnp.sum(arrived, axis=0, dtype=jnp.float32).astype(jnp.bfloat16)  9.64 us
    concatenate x3, local copies, waits for them, and re-layouts, conv_valid(): columns = jnp.concatenate(pieces, axis=-1)  6.5 us
    unnamed x57, local copies, waits for them, and re-layouts  6.16 us
  transfers between devices with their start and end apart: 3, of which 3 were waited for; matrix products, arithmetic and copies ran while one was open for 0% of the time, Pallas kernels for 0%

commit v1 on v0

v1 whole, which is shorter than its diff:
```python
import jax
import jax.numpy as jnp
import numpy as np
from jax import lax
from jax.experimental import pallas as pl
from jax.experimental.pallas import tpu as pltpu
from jax.sharding import PartitionSpec as P

F32 = jnp.float32
BF16 = jnp.bfloat16
ZC = 16
CH = 384
EXT = 16
TS = 10
SPAN = 4
STEM = EXT - 2
MID = EXT - 4
STEM_ROWS = STEM * EXT
MID_ROWS = MID * MID
TAPS = 9 * CH


def gathers():
    one = np.zeros((25 * 16, STEM_ROWS), np.float32)
    for ry in range(5):
        for rx in range(5):
            for j in range(16):
                y, x = 3 * (j // 4) + ry, 3 * (j % 4) + rx
                one[(ry * 5 + rx) * 16 + j, x * EXT + y] = 1
    two = np.zeros((16 * 32, MID_ROWS), np.float32)
    for ry in range(4):
        for rx in range(4):
            for j in range(25):
                y, x = 2 * (j // 5) + ry, 2 * (j % 5) + rx
                two[(ry * 4 + rx) * 32 + j, ((y % 3) * 3 + x % 3) * 16 + (y // 3) * 4 + x // 3] = 1
    skip = np.zeros((4 * 32, STEM_ROWS), np.float32)
    out = np.zeros((112, 4 * 32), np.float32)
    for y in range(TS):
        for x in range(TS):
            row = ((y % 2) * 2 + x % 2) * 32 + (y // 2) * 5 + x // 2
            skip[row, (x + 2) * EXT + y + 2] = 1
            out[y * TS + x, row] = 1
    return [jnp.asarray(a, BF16) for a in (one, two, skip, out)]


def dot(a, b):
    return jnp.dot(a, b, preferred_element_type=F32)


def activate(u, gain):
    half = 0.5 * (u * lax.rsqrt(jnp.mean(u * u, axis=-1, keepdims=True) + 1e-06) * gain)
    return half + half * jnp.tanh(half)


def inside(row, col, high, wide):
    return ((row >= 0) & (row < high) & (col >= 0) & (col < wide)).astype(F32)


def decode_kernel(
    info, field, w_in, b_in, gain_one, b_one, gain_two, b_two, to_one, to_two, to_skip, to_out,
    w_one, w_two, out, lhs, act_one, act_two, skip, middle, w_one_v, w_two_v, sems,
):
    copies = []
    for n, (src, dst) in enumerate(((w_one, w_one_v), (w_two, w_two_v))):
        for step in range(3):
            tap = 2 - step if n == 0 else step
            copy = pltpu.make_async_copy(
                src.at[pl.ds(tap * TAPS, TAPS)], dst.at[pl.ds(tap * TAPS, TAPS)], sems.at[n, tap]
            )
            copy.start()
            copies.append(copy)
    row0, col0, high, wide, first = info[0], info[1], info[2], info[3], info[4]

    lane = lax.broadcasted_iota(jnp.int32, (SPAN * EXT, EXT * ZC), 1)
    line = lax.broadcasted_iota(jnp.int32, (SPAN * EXT, EXT * ZC), 0)
    cells = field[...].astype(F32) * inside(
        row0 - 3 + (line & (EXT - 1)), col0 - 3 + lane // ZC, high, wide
    )
    rolled = [
        cells,
        pltpu.roll(pltpu.roll(cells, SPAN * EXT - 1, 0), 3 * ZC, 1),
        pltpu.roll(pltpu.roll(cells, SPAN * EXT - 2, 0), 6 * ZC, 1),
    ]
    for x in range(STEM):
        at = [pltpu.roll(r, (EXT * ZC - ZC * x) % (EXT * ZC), 1) if x else r for r in rolled]
        packed = jnp.where(lane < 3 * ZC, at[0], jnp.where(lane < 6 * ZC, at[1], at[2]))
        lhs[:, x] = packed.astype(BF16).reshape(SPAN, EXT, EXT * ZC)

    pos = lax.broadcasted_iota(jnp.int32, (STEM_ROWS, 1), 0)
    mask_one = inside(row0 - 2 + (pos & (EXT - 1)), col0 - 2 + (pos >> 4), high, wide)
    for f in range(SPAN):
        stem = b_in[...]
        for dt in range(3):
            if f + dt - 2 >= 0:
                left = lhs[f + dt - 2].reshape(STEM_ROWS, EXT * ZC)[:, : 9 * ZC]
                stem = stem + dot(left, w_in[pl.ds(dt * 9 * ZC, 9 * ZC), :])
        act = activate(stem, gain_one[...]) * mask_one
        if f < 2:
            act = act * (first + f >= 0).astype(F32)
        moved = dot(to_one[...], act.astype(BF16))
        act_one[f] = moved.astype(BF16).reshape(5, 5, 16, CH)
        if f >= 2:
            coarse = stem.astype(BF16)
            fine = (stem - coarse.astype(F32)).astype(BF16)
            skip[f - 2] = dot(to_skip[...], coarse) + dot(to_skip[...], fine) + b_two[...]

    for step in range(3):
        dt = 2 - step
        copies[step].wait()
        frames = 2 + dt
        left = jnp.concatenate(
            [
                act_one[0:frames, dy : dy + 3, dx : dx + 3].reshape(frames * MID_ROWS, CH)
                for dy in range(3)
                for dx in range(3)
            ],
            axis=-1,
        )
        part = dot(left, w_one_v[pl.ds(dt * TAPS, TAPS), :])
        rows = pl.ds((SPAN - frames) * MID_ROWS, frames * MID_ROWS)
        if step == 0:
            middle[...] = part
        else:
            middle[rows, :] += part
    spot = lax.broadcasted_iota(jnp.int32, (MID_ROWS, 1), 0)
    block = spot >> 4
    block_y = (block >= 3).astype(jnp.int32) + (block >= 6).astype(jnp.int32)
    mid_y = 3 * ((spot >> 2) & 3) + block_y
    mid_x = 3 * (spot & 3) + block - 3 * block_y
    mask_two = inside(row0 - 1 + mid_y, col0 - 1 + mid_x, high, wide)
    for f in range(SPAN):
        act = activate(middle[pl.ds(f * MID_ROWS, MID_ROWS), :] + b_one[...], gain_two[...]) * mask_two
        if f < 2:
            act = act * (first + f >= 0).astype(F32)
        act_two[f] = dot(to_two[...], act.astype(BF16)).astype(BF16).reshape(4, 4, 32, CH)

    total = skip[...].reshape(2 * 128, CH)
    for dt in range(3):
        copies[3 + dt].wait()
        left = jnp.concatenate(
            [
                act_two[dt : dt + 2, dy : dy + 2, dx : dx + 2].reshape(2 * 128, CH)
                for dy in range(3)
                for dx in range(3)
            ],
            axis=-1,
        )
        total = total + dot(left, w_two_v[pl.ds(dt * TAPS, TAPS), :])
    for f in range(2):
        live = first + 2 + f < info[5]
        final = jnp.where(live, total[f * 128 : (f + 1) * 128], 0.0).astype(BF16)
        out[f] = dot(to_out[...], final)[: TS * TS].astype(BF16)


def decode(info, field, w_in, b_in, gain_one, w_one, b_one, gain_two, w_two, b_two):
    vmem = pl.BlockSpec(memory_space=pltpu.VMEM)
    hbm = pl.BlockSpec(memory_space=pl.ANY)
    row = lambda v: v.reshape(1, CH)
    return pl.pallas_call(
        decode_kernel,
        out_shape=jax.ShapeDtypeStruct((2, TS * TS, CH), BF16),
        in_specs=[pl.BlockSpec(memory_space=pltpu.SMEM)] + [vmem] * 11 + [hbm] * 2,
        out_specs=vmem,
        scratch_shapes=[
            pltpu.VMEM((SPAN, STEM, EXT, EXT * ZC), BF16),
            pltpu.VMEM((SPAN, 5, 5, 16, CH), BF16),
            pltpu.VMEM((SPAN, 4, 4, 32, CH), BF16),
            pltpu.VMEM((2, 128, CH), F32),
            pltpu.VMEM((SPAN * MID_ROWS, CH), F32),
            pltpu.VMEM((3 * TAPS, CH), BF16),
            pltpu.VMEM((3 * TAPS, CH), BF16),
            pltpu.SemaphoreType.DMA((2, 3)),
        ],
        compiler_params=pltpu.CompilerParams(vmem_limit_bytes=48 << 20),
        cost_estimate=pl.CostEstimate(
            flops=2 * 27 * CH * CH * (SPAN * MID_ROWS + 200), bytes_accessed=16 << 20, transcendentals=0
        ),
    )(
        info, field, w_in, row(b_in), row(gain_one), row(b_one), row(gain_two), row(b_two),
        *gathers(), w_one, w_two,
    )


def slot_info(resolution, frame_counts, tile_rows, tile_cols, decoder_list):
    mine = lax.axis_index("video") * lax.axis_size("tile") + lax.axis_index("tile")
    match = decoder_list == mine
    pick = lambda table: jnp.sum(jnp.where(match, table, 0))
    high = (2 + 2 * pick(jnp.broadcast_to(resolution[:, None], match.shape))) * TS - 3
    counts = pick(jnp.broadcast_to(frame_counts[:, None], match.shape))
    wide = lax.axis_size("tile") // 4 * TS - 4
    first = 2 * lax.axis_index("section") - 2
    return jnp.stack(
        [pick(tile_rows), pick(tile_cols), high, jnp.int32(wide), first, counts]
    ).astype(jnp.int32)


def local(
    latent, resolution, frame_counts, tile_rows, tile_cols, decoder_list,
    w_in, b_in, gain_one, w_one, b_one, gain_two, w_two, b_two,
):
    tile_count, video_count = lax.axis_size("tile"), lax.axis_size("video")
    slot = lax.axis_index("tile")
    own = lax.dynamic_slice(decoder_list, (2 * lax.axis_index("video"), slot), (2, 1))
    peers = jnp.arange(video_count * tile_count, dtype=jnp.int32)
    owned = latent[:, 0].reshape(2, 2 * EXT, EXT * ZC).astype(BF16)
    sent = jnp.where((peers == own[0, 0])[:, None, None], owned[0], jnp.zeros((), BF16))
    sent = jnp.where((peers == own[1, 0])[:, None, None], owned[1], sent)
    got = lax.all_to_all(sent, ("video", "tile"), split_axis=0, concat_axis=0, tiled=True)
    frames = jnp.sum(got, axis=0, dtype=F32).astype(BF16)
    earlier = lax.ppermute(frames, "section", [(0, 1)])
    field = jnp.concatenate([earlier, frames], axis=0)
    info = slot_info(resolution, frame_counts, tile_rows, tile_cols, decoder_list)
    decoded = decode(info, field, w_in, b_in, gain_one, w_one, b_one, gain_two, w_two, b_two)
    return decoded[None, None]


def solution(mesh):
    return jax.shard_map(
        local,
        mesh=mesh,
        in_specs=(P("video", "tile", "section", None, None),) + (P(),) * 13,
        out_specs=P("video", "tile", "section", None, None),
        check_vma=False,
    )
```

time: 282 us -> 65.7 us (0.23)
  the two profiles are of different devices: /device:TPU:0 before, /device:TPU:1 now
where the time goes in v1:
time: 65.7 us; the launch traced here: 65 us
  waiting for transfers between devices  18.9 us (29%)
  starting transfers between devices  15 us (23%)
  Pallas kernels  13.4 us (20%)
  local copies, waits for them, and re-layouts  12 us (18%)
  other arithmetic  5.13 us (8%)
  between operations  0.7 us (1%)
    all_to_all x1, waiting for transfers between devices, local(): lax.all_to_all(sent, ('video', 'tile'), split_axis=0, concat_axis=0, tile...  18.9 us
    pallas_call x1, Pallas kernels, decode(): pl.pallas_call(decode_kernel, out_shape=jax.ShapeDtypeStruct((2, TS * TS,...  13.4 us
    all_to_all x1, starting transfers between devices, local(): lax.all_to_all(sent, ('video', 'tile'), split_axis=0, concat_axis=0, tile...  12.3 us
    unnamed x10, local copies, waits for them, and re-layouts  4.43 us
    reshape x5, local copies, waits for them, and re-layouts, decode(): row = lambda v: v.reshape(1, CH)  3.42 us
    ppermute x1, starting transfers between devices, local(): earlier = lax.ppermute(frames, 'section', [(0, 1)])  2.65 us
    another operation x1, local copies, waits for them, and re-layouts, slot_info(): jnp.stack([pick(tile_rows), pick(tile_cols), high, jnp.int32(wide), first...  1.98 us
    reduce_sum x1, other arithmetic, slot_info(): pick = lambda table: jnp.sum(jnp.where(match, table, 0))  1.57 us
  transfers between devices with their start and end apart: 2, of which 1 were waited for; matrix products, arithmetic and copies ran while one was open for 11% of the time, Pallas kernels for 0%

profile of v1, /device:TPU:1, one launch (start us, length us, event | category | flops | bytes accessed | tf_op | source)
XLA Modules:
  0.0 65.0 jit_solution(4014247060346954792)
XLA Ops:
  0.0 0.8 %dynamic_slice.3 = s32[2,1]{1,0:T(2,128)S(1)} dynamic-slice(s32[4,32]{1,0:T(4,128)} %param.23, s32[]{:T(128)S(6)} %select_n.31, s32[]{:T(128)S(6)} %select_n.32), dynamic_slice_sizes={2,1} | dynamic-slice | bytes 20 | tf_op jit(solution)/shard_map/dynamic_slice | solution.py:203
  0.8 0.6 fusion.1
  1.4 0.8 %convert_element_type.6 = bf16[2,1,2,16,256]{4,3,2,1,0:T(8,128)(2,1)S(1)} convert(f32[2,1,2,16,256]{4,3,2,1,0:T(8,128)} %param.18) | non-fusion elementwise | flops 16384 | bytes 98304 | tf_op jit(solution)/shard_map/convert_element_type | solution.py:205
  2.2 1.3 %iota_compare_fusion = (pred[64]{0:T(512)(128)(4,1)S(1)}, pred[64]{0:T(512)(128)(4,1)S(1)}) fusion(s32[]{:T(128)} %bitcast.7, s32[]{:T(128)} %bitcast.5), kind=kLoop, calls=%fused_computation.7 | loop fusion | flops 128 | bytes 136 | tf_op jit(solution)/shard_map/eq | solution.py:206
  3.5 1.2 %select_select_fusion = bf16[64,32,256]{2,1,0:T(8,128)(2,1)} fusion(pred[64]{0:T(512)(128)(4,1)S(1)} %get-tuple-element.13, pred[64]{0:T(512)(128)(4,1)S(1)} %get-tuple-element.14, bf16[32,256]{1,0:T(8,128)(2,1)S(1)} %bitcast.12, bf16[32,256]{1,0:T(8,128)(2,1)S(1)} %bitcast.11), kind=kLoop, calls=%fused_computation | loop fusion | flops 1048576 | bytes 1081472 | tf_op jit(solution)/shard_map/jit(_where)/select_n | solution.py:207
  4.8 12.3 %all-to-all-start = ((bf16[64,32,256]{2,1,0:T(8,128)(2,1)}), bf16[64,32,256]{2,1,0:T(8,128)(2,1)S(1)}, u32[]{:S(2)}, u32[]{:S(2)}) async-start(bf16[64,32,256]{2,1,0:T(8,128)(2,1)} %select_select_fusion), calls=%async_computation | async-start | bytes 2097152 | tf_op jit(solution)/shard_map/all_to_all | solution.py:208
  17.1 18.9 %all-to-all-done = bf16[64,32,256]{2,1,0:T(8,128)(2,1)S(1)} async-done(((bf16[64,32,256]{2,1,0:T(8,128)(2,1)}), bf16[64,32,256]{2,1,0:T(8,128)(2,1)S(1)}, u32[]{:S(2)}, u32[]{:S(2)}) %all-to-all-start) | async-done | bytes 1048608 | tf_op jit(solution)/shard_map/all_to_all | solution.py:208
  36.0 0.2 reduce_sum.52
  36.1 2.7 %collective-permute-start = (bf16[32,256]{1,0:T(8,128)(2,1)S(1)}, bf16[32,256]{1,0:T(8,128)(2,1)S(1)}, u32[]{:S(2)}, u32[]{:S(2)}) collective-permute-start(bf16[32,256]{1,0:T(8,128)(2,1)S(1)} %reduce_sum.52), channel_id=1, source_target_pairs={{0,1},{2,3},{4,5},{6,7},{8,9},{10,11},{12,13},{14,15},{16,17},{18,... | collective-permute-start | bytes 49160 | tf_op jit(solution)/shard_map/ppermute | solution.py:210
  38.8 1.6 %select_reduce_fusion = (s32[]{:T(128)}, s32[]{:T(128)}, s32[]{:T(128)}, s32[]{:T(128)}) fusion(s32[4]{0:T(128)} %param.20, s32[4]{0:T(128)} %param.19, s32[4,32]{1,0:T(4,128)} %param.22, s32[4,32]{1,0:T(4,128)} %param.21, s32[4,32]{1,0:T(4,128)} %param.23, s32[]{:T(128)S(6)} %add.14), kind=kLoop, calls=%fused_computation.2 | loop fusion | flops 1148 | bytes 1588 | tf_op jit(solution)/shard_map/reduce_sum | solution.py:187
  41.0 0.7 %reshape.30.b_in = f32[1,384]{1,0:T(1,128)S(1)} reshape(f32[384]{0:T(512)} %param.25) | data formatting | bytes 3072 | tf_op jit(solution)/shard_map/reshape | solution.py:158
  41.7 0.7 %reshape.31.gain_one = f32[1,384]{1,0:T(1,128)S(1)} reshape(f32[384]{0:T(512)} %param.26) | data formatting | bytes 3072 | tf_op jit(solution)/shard_map/reshape | solution.py:158
  42.4 0.7 %reshape.32.b_one = f32[1,384]{1,0:T(1,128)S(1)} reshape(f32[384]{0:T(512)} %param.28) | data formatting | bytes 3072 | tf_op jit(solution)/shard_map/reshape | solution.py:158
  43.1 0.7 %reshape.33.gain_two = f32[1,384]{1,0:T(1,128)S(1)} reshape(f32[384]{0:T(512)} %param.29) | data formatting | bytes 3072 | tf_op jit(solution)/shard_map/reshape | solution.py:158
  43.7 0.7 %reshape.34.b_two = f32[1,384]{1,0:T(1,128)S(1)} reshape(f32[384]{0:T(512)} %param.31) | data formatting | bytes 3072 | tf_op jit(solution)/shard_map/reshape | solution.py:158
  44.4 2.0 %stack.23.info = s32[6]{0:T(128)S(1)} concatenate(s32[1]{0:T(128)} %bitcast, s32[1]{0:T(128)} %bitcast.1, s32[1]{0:T(128)} %bitcast.2, s32[1]{0:T(128)} %constant.37.clone.1, s32[1]{0:T(128)} %bitcast.3, s32[1]{0:T(128)} %bitcast.4), dimensions={0} | concatenate | bytes 48 | tf_op jit(solution)/shard_map/stack | solution.py:192
  46.4 0.0 collective-permute-done
  46.4 0.0 copy-start
  46.4 1.0 %copy-done = bf16[432,384]{1,0:T(8,128)(2,1)S(1)} copy-done((bf16[432,384]{1,0:T(8,128)(2,1)S(1)}, bf16[432,384]{1,0:T(8,128)(2,1)}, u32[]{:S(2)}) %copy-start) | copy-done | bytes 331800
  47.4 0.0 copy-start.1
  47.4 0.9 %copy-done.1 = bf16[512,144]{1,0:T(8,128)(2,1)S(1)} copy-done((bf16[512,144]{1,0:T(8,128)(2,1)S(1)}, bf16[512,144]{1,0:T(8,128)(2,1)}, u32[]{:S(2)}) %copy-start.1) | copy-done | bytes 147480
  48.3 0.0 copy-start.2
  48.3 0.9 %copy-done.2 = bf16[400,224]{1,0:T(8,128)(2,1)S(1)} copy-done((bf16[400,224]{1,0:T(8,128)(2,1)S(1)}, bf16[400,224]{1,0:T(8,128)(2,1)}, u32[]{:S(2)}) %copy-start.2) | copy-done | bytes 179224
  49.3 0.0 copy-start.3
  49.3 0.8 %copy-done.3 = bf16[128,224]{1,0:T(8,128)(2,1)S(1)} copy-done((bf16[128,224]{1,0:T(8,128)(2,1)S(1)}, bf16[128,224]{1,0:T(8,128)(2,1)}, u32[]{:S(2)}) %copy-start.3) | copy-done | bytes 57368
  50.1 0.0 copy-start.4
  50.1 0.7 %copy-done.4 = bf16[112,128]{1,0:T(8,128)(2,1)S(1)} copy-done((bf16[112,128]{1,0:T(8,128)(2,1)S(1)}, bf16[112,128]{1,0:T(8,128)(2,1)}, u32[]{:S(2)}) %copy-start.4) | copy-done | bytes 28696
  50.9 13.4 %shard_map.172 = bf16[2,100,384]{2,1,0:T(8,128)(2,1)S(1)} custom-call(s32[6]{0:T(128)S(1)} %stack.23.info, bf16[64,256]{1,0:T(8,128)(2,1)S(1)} %pad_maximum_fusion.field, bf16[432,384]{1,0:T(8,128)(2,1)S(1)} %copy-done, f32[1,384]{1,0:T(1,128)S(1)} %reshape.30.b_in, f32[1,384]{1,0:T(1,128)S(1)} %reshape.31.gain_one, f32[1,384]{1,0:T(1,128)S(1)} %reshape.32.b_one, ...), custom_call_target="tpu_custom_call" | custom-call | flops 6178996224 | bytes 16777216 | tf_op jit(solution)/shard_map/pallas_call | solution.py:159
  64.3 0.8 %copy.20 = bf16[1,1,2,100,384]{4,2,3,1,0:T(2,128)(2,1)} copy(bf16[1,1,2,100,384]{4,3,2,1,0:T(8,128)(2,1)S(1)} %bitcast.10) | data formatting | bytes 307200 | tf_op jit(solution)/shard_map/broadcast_in_dim | solution.py:214
  (2 shorter events, 0.0 us)
Async XLA Ops:
  4.8 31.2 %all-to-all-start = ((bf16[64,32,256]{2,1,0:T(8,128)(2,1)}), bf16[64,32,256]{2,1,0:T(8,128)(2,1)S(1)}, u32[]{:S(2)}, u32[]{:S(2)}) async-start(bf16[64,32,256]{2,1,0:T(8,128)(2,1)} %select_select_fusion), calls=%async_computation | async-start | bytes 2097152 | tf_op jit(solution)/shard_map/all_to_all | solution.py:208
  36.1 10.3 %collective-permute-start = (bf16[32,256]{1,0:T(8,128)(2,1)S(1)}, bf16[32,256]{1,0:T(8,128)(2,1)S(1)}, u32[]{:S(2)}, u32[]{:S(2)}) collective-permute-start(bf16[32,256]{1,0:T(8,128)(2,1)S(1)} %reduce_sum.52), channel_id=1, source_target_pairs={{0,1},{2,3},{4,5},{6,7},{8,9},{10,11},{12,13},{14,15},{16,17},{18,... | collective-permute-start | bytes 49160 | tf_op jit(solution)/shard_map/ppermute | solution.py:210
  46.4 1.0 %copy-start = (bf16[432,384]{1,0:T(8,128)(2,1)S(1)}, bf16[432,384]{1,0:T(8,128)(2,1)}, u32[]{:S(2)}) copy-start(bf16[432,384]{1,0:T(8,128)(2,1)} %w_in.1) | copy-start | bytes 995332
  47.4 0.9 %copy-start.1 = (bf16[512,144]{1,0:T(8,128)(2,1)S(1)}, bf16[512,144]{1,0:T(8,128)(2,1)}, u32[]{:S(2)}) copy-start(bf16[512,144]{1,0:T(8,128)(2,1)} %constant.42.clone.to_two) | copy-start | bytes 442372
  48.3 0.9 %copy-start.2 = (bf16[400,224]{1,0:T(8,128)(2,1)S(1)}, bf16[400,224]{1,0:T(8,128)(2,1)}, u32[]{:S(2)}) copy-start(bf16[400,224]{1,0:T(8,128)(2,1)} %constant.41.clone.to_one) | copy-start | bytes 537604
  49.3 0.8 %copy-start.3 = (bf16[128,224]{1,0:T(8,128)(2,1)S(1)}, bf16[128,224]{1,0:T(8,128)(2,1)}, u32[]{:S(2)}) copy-start(bf16[128,224]{1,0:T(8,128)(2,1)} %constant.43.clone.to_skip) | copy-start | bytes 172036
  50.1 0.7 %copy-start.4 = (bf16[112,128]{1,0:T(8,128)(2,1)S(1)}, bf16[112,128]{1,0:T(8,128)(2,1)}, u32[]{:S(2)}) copy-start(bf16[112,128]{1,0:T(8,128)(2,1)} %constant.44.clone.to_out) | copy-start | bytes 86020

commit v2 on v1

--- a/solution.py
+++ b/solution.py
@@ -57,9 +57,15 @@
 
 
 def decode_kernel(
-    info, field, w_in, b_in, gain_one, b_one, gain_two, b_two, to_one, to_two, to_skip, to_out,
-    w_one, w_two, out, lhs, act_one, act_two, skip, middle, w_one_v, w_two_v, sems,
+    info, here, across, far, vectors, w_in_h, to_one_h, to_two_h, to_skip_h, to_out_h, w_one, w_two, out,
+    w_in, to_one, to_two, to_skip, to_out, lhs, act_one, act_two, skip, middle, w_one_v, w_two_v, small, sems,
 ):
+    tables = []
+    for n, (src, dst) in enumerate(
+        ((w_in_h, w_in), (to_one_h, to_one), (to_two_h, to_two), (to_skip_h, to_skip), (to_out_h, to_out))
+    ):
+        tables.append(pltpu.make_async_copy(src, dst, small.at[n]))
+        tables[n].start()
     copies = []
     for n, (src, dst) in enumerate(((w_one, w_one_v), (w_two, w_two_v))):
         for step in range(3):
@@ -69,11 +75,15 @@
             )
             copy.start()
             copies.append(copy)
-    row0, col0, high, wide, first = info[0], info[1], info[2], info[3], info[4]
+    row0, col0, high, count, section = info[0], info[1], (2 + 2 * info[2]) * TS - 3, info[3], info[4]
+    wide, first = info[5], 2 * section - 2
+    b_in, gain_one, b_one, gain_two, b_two = [vectors[n : n + 1, :] for n in range(5)]
 
     lane = lax.broadcasted_iota(jnp.int32, (SPAN * EXT, EXT * ZC), 1)
     line = lax.broadcasted_iota(jnp.int32, (SPAN * EXT, EXT * ZC), 0)
-    cells = field[...].astype(F32) * inside(
+    own = here[0].astype(F32) + far[1].astype(F32)
+    other = (across[0].astype(F32) + far[0].astype(F32)) * section.astype(F32)
+    cells = jnp.concatenate([other, own], axis=0) * inside(
         row0 - 3 + (line & (EXT - 1)), col0 - 3 + lane // ZC, high, wide
     )
     rolled = [
@@ -86,15 +96,17 @@
         packed = jnp.where(lane < 3 * ZC, at[0], jnp.where(lane < 6 * ZC, at[1], at[2]))
         lhs[:, x] = packed.astype(BF16).reshape(SPAN, EXT, EXT * ZC)
 
+    for table in tables:
+        table.wait()
     pos = lax.broadcasted_iota(jnp.int32, (STEM_ROWS, 1), 0)
     mask_one = inside(row0 - 2 + (pos & (EXT - 1)), col0 - 2 + (pos >> 4), high, wide)
     for f in range(SPAN):
-        stem = b_in[...]
+        stem = b_in
         for dt in range(3):
             if f + dt - 2 >= 0:
                 left = lhs[f + dt - 2].reshape(STEM_ROWS, EXT * ZC)[:, : 9 * ZC]
                 stem = stem + dot(left, w_in[pl.ds(dt * 9 * ZC, 9 * ZC), :])
-        act = activate(stem, gain_one[...]) * mask_one
+        act = activate(stem, gain_one) * mask_one
         if f < 2:
             act = act * (first + f >= 0).astype(F32)
         moved = dot(to_one[...], act.astype(BF16))
@@ -102,7 +114,7 @@
         if f >= 2:
             coarse = stem.astype(BF16)
             fine = (stem - coarse.astype(F32)).astype(BF16)
-            skip[f - 2] = dot(to_skip[...], coarse) + dot(to_skip[...], fine) + b_two[...]
+            skip[f - 2] = dot(to_skip[...], coarse) + dot(to_skip[...], fine) + b_two
 
     for step in range(3):
         dt = 2 - step
@@ -129,7 +141,7 @@
     mid_x = 3 * (spot & 3) + block - 3 * block_y
     mask_two = inside(row0 - 1 + mid_y, col0 - 1 + mid_x, high, wide)
     for f in range(SPAN):
-        act = activate(middle[pl.ds(f * MID_ROWS, MID_ROWS), :] + b_one[...], gain_two[...]) * mask_two
+        act = activate(middle[pl.ds(f * MID_ROWS, MID_ROWS), :] + b_one, gain_two) * mask_two
         if f < 2:
             act = act * (first + f >= 0).astype(F32)
         act_two[f] = dot(to_two[...], act.astype(BF16)).astype(BF16).reshape(4, 4, 32, CH)
@@ -147,21 +159,22 @@
         )
         total = total + dot(left, w_two_v[pl.ds(dt * TAPS, TAPS), :])
     for f in range(2):
-        live = first + 2 + f < info[5]
+        live = first + 2 + f < count
         final = jnp.where(live, total[f * 128 : (f + 1) * 128], 0.0).astype(BF16)
         out[f] = dot(to_out[...], final)[: TS * TS].astype(BF16)
 
 
-def decode(info, field, w_in, b_in, gain_one, w_one, b_one, gain_two, w_two, b_two):
+def decode(info, here, across, far, vectors, w_in, w_one, w_two):
     vmem = pl.BlockSpec(memory_space=pltpu.VMEM)
     hbm = pl.BlockSpec(memory_space=pl.ANY)
-    row = lambda v: v.reshape(1, CH)
+    tables = [w_in, *gathers()]
     return pl.pallas_call(
         decode_kernel,
         out_shape=jax.ShapeDtypeStruct((2, TS * TS, CH), BF16),
-        in_specs=[pl.BlockSpec(memory_space=pltpu.SMEM)] + [vmem] * 11 + [hbm] * 2,
+        in_specs=[pl.BlockSpec(memory_space=pltpu.SMEM)] + [vmem] * 4 + [hbm] * 7,
         out_specs=vmem,
-        scratch_shapes=[
+        scratch_shapes=[pltpu.VMEM(t.shape, BF16) for t in tables]
+        + [
             pltpu.VMEM((SPAN, STEM, EXT, EXT * ZC), BF16),
             pltpu.VMEM((SPAN, 5, 5, 16, CH), BF16),
             pltpu.VMEM((SPAN, 4, 4, 32, CH), BF16),
@@ -169,49 +182,59 @@
             pltpu.VMEM((SPAN * MID_ROWS, CH), F32),
             pltpu.VMEM((3 * TAPS, CH), BF16),
             pltpu.VMEM((3 * TAPS, CH), BF16),
+            pltpu.SemaphoreType.DMA((5,)),
             pltpu.SemaphoreType.DMA((2, 3)),
         ],
         compiler_params=pltpu.CompilerParams(vmem_limit_bytes=48 << 20),
         cost_estimate=pl.CostEstimate(
             flops=2 * 27 * CH * CH * (SPAN * MID_ROWS + 200), bytes_accessed=16 << 20, transcendentals=0
         ),
-    )(
-        info, field, w_in, row(b_in), row(gain_one), row(b_one), row(gain_two), row(b_two),
-        *gathers(), w_one, w_two,
-    )
-
-
-def slot_info(resolution, frame_counts, tile_rows, tile_cols, decoder_list):
-    mine = lax.axis_index("video") * lax.axis_size("tile") + lax.axis_index("tile")
+    )(info, here, across, far, vectors, *tables, w_one, w_two)
+
+
+def slot_info(resolution, frame_counts, tile_rows, tile_cols, decoder_list, mine):
     match = decoder_list == mine
-    pick = lambda table: jnp.sum(jnp.where(match, table, 0))
-    high = (2 + 2 * pick(jnp.broadcast_to(resolution[:, None], match.shape))) * TS - 3
-    counts = pick(jnp.broadcast_to(frame_counts[:, None], match.shape))
-    wide = lax.axis_size("tile") // 4 * TS - 4
-    first = 2 * lax.axis_index("section") - 2
-    return jnp.stack(
-        [pick(tile_rows), pick(tile_cols), high, jnp.int32(wide), first, counts]
-    ).astype(jnp.int32)
+    wide = lambda t: jnp.broadcast_to(t[:, None], match.shape)
+    tables = jnp.stack([tile_rows, tile_cols, wide(resolution), wide(frame_counts)])
+    picked = jnp.sum(jnp.where(match[None], tables, 0), axis=(1, 2))
+    place = jnp.array([0, lax.axis_size("tile") // 4 * TS - 4], jnp.int32)
+    place = place + jnp.array([1, 0], jnp.int32) * lax.axis_index("section")
+    return jnp.concatenate([picked, place]).astype(jnp.int32)
 
 
 def local(
     latent, resolution, frame_counts, tile_rows, tile_cols, decoder_list,
     w_in, b_in, gain_one, w_one, b_one, gain_two, w_two, b_two,
 ):
-    tile_count, video_count = lax.axis_size("tile"), lax.axis_size("video")
-    slot = lax.axis_index("tile")
-    own = lax.dynamic_slice(decoder_list, (2 * lax.axis_index("video"), slot), (2, 1))
-    peers = jnp.arange(video_count * tile_count, dtype=jnp.int32)
-    owned = latent[:, 0].reshape(2, 2 * EXT, EXT * ZC).astype(BF16)
-    sent = jnp.where((peers == own[0, 0])[:, None, None], owned[0], jnp.zeros((), BF16))
-    sent = jnp.where((peers == own[1, 0])[:, None, None], owned[1], sent)
-    got = lax.all_to_all(sent, ("video", "tile"), split_axis=0, concat_axis=0, tiled=True)
-    frames = jnp.sum(got, axis=0, dtype=F32).astype(BF16)
-    earlier = lax.ppermute(frames, "section", [(0, 1)])
-    field = jnp.concatenate([earlier, frames], axis=0)
-    info = slot_info(resolution, frame_counts, tile_rows, tile_cols, decoder_list)
-    decoded = decode(info, field, w_in, b_in, gain_one, w_one, b_one, gain_two, w_two, b_two)
-    return decoded[None, None]
+    tiles = lax.axis_size("tile")
+    video, tile = lax.axis_index("video"), lax.axis_index("tile")
+    mine = video * tiles + tile
+    flip = lambda a, by, count=tiles: lax.ppermute(a, "tile", [(i, i ^ by) for i in range(count)])
+    unit = (2 * EXT, EXT * ZC)
+
+    first = flip(latent, 1)
+    have = jnp.concatenate([latent, first]).astype(BF16).reshape(4, *unit)
+    have = jnp.concatenate([have, flip(have, 2)])
+    have = jnp.concatenate([have, flip(have, 6)])
+    hops = np.array([far ^ near ^ core for far in (0, 6) for near in (0, 2) for core in (0, 1)], np.int32)
+    slots = (tile ^ hops)[:, None] == jnp.arange(tiles, dtype=jnp.int32)
+    names = lax.dynamic_slice(decoder_list, (2 * video, 0), (2, tiles))
+    names = jnp.sum(jnp.where(slots[:, None], names[None], 0), axis=-1).reshape(16)
+
+    rows = np.array([row ^ group for row in (0, 24, 8, 16) for group in (0, tiles)], np.int32)
+    match = (mine ^ rows)[:, None] == names[None, :]
+    kept = jnp.sum(
+        jnp.where(match[:, :, None, None], have[None], jnp.zeros((), BF16)), axis=1, dtype=F32
+    ).astype(BF16)
+    kept = kept[:4] + flip(kept[4:], 8, 16)
+    here = kept[:2] + flip(kept[2:], 24, 16)
+    across = lax.ppermute(here, "section", [(0, 1), (1, 0)])
+    outward = jnp.stack([here[1], across[1]])
+    far = lax.ppermute(outward, ("video", "section"), [(z, z ^ 3) for z in range(4)])
+
+    info = slot_info(resolution, frame_counts, tile_rows, tile_cols, decoder_list, mine)
+    vectors = jnp.stack([b_in, gain_one, b_one, gain_two, b_two])
+    return decode(info, here, across, far, vectors, w_in, w_one, w_two)[None, None]
 
 
 def solution(mesh):

time: 65.7 us -> 48.5 us (0.74)
  the two profiles are of different devices: /device:TPU:1 before, /device:TPU:0 now
where the time goes in v2:
time: 48.5 us; the launch traced here: 47.6 us
  starting transfers between devices  15.3 us (32%)
  Pallas kernels  13.2 us (27%)
  waiting for transfers between devices  10.5 us (22%)
  other arithmetic  5.22 us (11%)
  local copies, waits for them, and re-layouts  3.18 us (7%)
    pallas_call x1, Pallas kernels, decode(): pl.pallas_call(decode_kernel, out_shape=jax.ShapeDtypeStruct((2, TS * TS,...  13.2 us
    ppermute x5, starting transfers between devices, local(): lax.ppermute(a, 'tile', [(i, i ^ by) for i in range(count)])  9.52 us
    ppermute x5, waiting for transfers between devices, local(): lax.ppermute(a, 'tile', [(i, i ^ by) for i in range(count)])  8.75 us
    ppermute x1, starting transfers between devices, local(): lax.ppermute(outward, ('video', 'section'), [(z, z ^ 3) for z in range(4)])  3.77 us
    ppermute x1, starting transfers between devices, local(): across = lax.ppermute(here, 'section', [(0, 1), (1, 0)])  2.03 us
    ppermute x1, waiting for transfers between devices, local(): lax.ppermute(outward, ('video', 'section'), [(z, z ^ 3) for z in range(4)])  1.71 us
    another operation x2, local copies, waits for them, and re-layouts, slot_info(): jnp.stack([tile_rows, tile_cols, wide(resolution), wide(frame_counts)])  1.45 us
    another operation x1, other arithmetic  0.98 us
  transfers between devices with their start and end apart: 7, of which 5 were waited for; matrix products, arithmetic and copies ran while one was open for 13% of the time, Pallas kernels for 0%

profile of v2, /device:TPU:0, one launch (start us, length us, event | category | flops | bytes accessed | tf_op | source)
XLA Modules:
  0.0 47.6 jit_solution(7104730141849960270)
XLA Ops:
  0.0 0.0 copy-start.2
  0.0 0.0 copy-start.6
  0.0 0.0 copy-start.7
  0.0 0.0 copy-start.8
  0.0 0.0 copy-start.9
  0.1 0.0 copy-start
  0.1 1.0 %convert.14 = bf16[2,1,2,16,256]{4,3,2,1,0:T(8,128)(2,1)S(1)} convert(f32[2,1,2,16,256]{4,3,2,1,0:T(8,128)} %param.22) | non-fusion elementwise | flops 16384 | bytes 98304 | tf_op jit(solution)/shard_map/convert.4
  1.0 0.0 collective-permute-start
  1.1 0.7 %broadcast_xor_fusion = s32[8]{0:T(128)S(1)} fusion(s32[8]{0:T(128)} %constant.41.clone, s32[]{:T(128)S(6)} %axis_index.36), kind=kLoop, calls=%fused_computation.15 | loop fusion | flops 8 | bytes 68 | tf_op jit(solution)/shard_map/xor | solution.py:220
  1.7 0.1 iota_compare_fusion
  1.8 0.7 %broadcast_xor_fusion.1 = s32[8]{0:T(128)S(1)} fusion(s32[8]{0:T(128)} %constant.42.clone, s32[]{:T(128)S(6)} %add.15), kind=kLoop, calls=%fused_computation.16 | loop fusion | flops 8 | bytes 68 | tf_op jit(solution)/shard_map/xor | solution.py:225
  2.5 0.7 %constant_dynamic-slice_fusion = s32[2,32]{1,0:T(2,128)S(1)} fusion(s32[4,32]{1,0:T(4,128)} %param.27, s32[]{:T(128)S(6)} %select_n.16), kind=kLoop, calls=%fused_computation.17 | loop fusion | bytes 516 | tf_op jit(solution)/shard_map/dynamic_slice | solution.py:221
  3.1 0.0 collective-permute-done
  3.2 1.7 %collective-permute-start.1 = (bf16[4,32,256]{2,1,0:T(8,128)(2,1)S(1)}, bf16[4,32,256]{2,1,0:T(8,128)(2,1)S(1)}, u32[]{:S(2)}, u32[]{:S(2)}) collective-permute-start(bf16[4,32,256]{2,1,0:T(8,128)(2,1)S(1)} %pad_maximum_fusion.2), channel_id=1, source_target_pairs={{0,4},{2,6},{4,0},{6,2},{8,12},{10,14},{12,8},{14,10},{16,20},{18,... | collective-permute-start | bytes 196616 | tf_op jit(solution)/shard_map/ppermute | solution.py:212
  4.8 0.1 select_reduce_fusion.1
  5.0 0.1 copy.25
  5.1 0.1 eq.48
  5.1 2.6 %collective-permute-done.1 = bf16[4,32,256]{2,1,0:T(8,128)(2,1)S(1)} collective-permute-done((bf16[4,32,256]{2,1,0:T(8,128)(2,1)S(1)}, bf16[4,32,256]{2,1,0:T(8,128)(2,1)S(1)}, u32[]{:S(2)}, u32[]{:S(2)}) %collective-permute-start.1) | collective-permute-done | bytes 65568 | tf_op jit(solution)/shard_map/ppermute | solution.py:212
  7.7 2.9 %collective-permute-start.2 = (bf16[8,32,256]{2,1,0:T(8,128)(2,1)S(1)}, bf16[8,32,256]{2,1,0:T(8,128)(2,1)S(1)}, u32[]{:S(2)}, u32[]{:S(2)}) collective-permute-start(bf16[8,32,256]{2,1,0:T(8,128)(2,1)S(1)} %pad_maximum_fusion.1), channel_id=1, source_target_pairs={{0,12},{2,14},{4,8},{6,10},{8,4},{10,6},{12,0},{14,2},{16,28},{18,... | collective-permute-start | bytes 393224 | tf_op jit(solution)/shard_map/ppermute | solution.py:212
  10.7 0.1 broadcast_compare_fusion
  10.8 3.4 %collective-permute-done.2 = bf16[8,32,256]{2,1,0:T(8,128)(2,1)S(1)} collective-permute-done((bf16[8,32,256]{2,1,0:T(8,128)(2,1)S(1)}, bf16[8,32,256]{2,1,0:T(8,128)(2,1)S(1)}, u32[]{:S(2)}, u32[]{:S(2)}) %collective-permute-start.2) | collective-permute-done | bytes 131104 | tf_op jit(solution)/shard_map/ppermute | solution.py:212
  14.2 0.3 select_reduce_fusion
  14.5 3.6 %collective-permute-start.3 = (bf16[4,32,256]{2,1,0:T(8,128)(2,1)S(1)}, bf16[4,32,256]{2,1,0:T(8,128)(2,1)S(1)}, u32[]{:S(2)}, u32[]{:S(2)}) collective-permute-start(bf16[4,32,256]{2,1,0:T(8,128)(2,1)S(1)} %slice.25), channel_id=1, source_target_pairs={{0,16},{2,18},{4,20},{6,22},{8,24},{10,26},{12,28},{14,30},{16,0},... | collective-permute-start | bytes 196616 | tf_op jit(solution)/shard_map/ppermute | solution.py:212
  18.1 0.7 %broadcast_compare_fusion.1 = pred[4,32]{1,0:T(4,128)(4,1)S(1)} fusion(s32[4,32]{1,0:T(4,128)} %param.27, s32[]{:T(128)S(6)} %add.15), kind=kLoop, calls=%fused_computation.12 | loop fusion | flops 128 | bytes 644 | tf_op jit(solution)/shard_map/eq | solution.py:196
  18.8 1.9 %collective-permute-done.3 = bf16[4,32,256]{2,1,0:T(8,128)(2,1)S(1)} collective-permute-done((bf16[4,32,256]{2,1,0:T(8,128)(2,1)S(1)}, bf16[4,32,256]{2,1,0:T(8,128)(2,1)S(1)}, u32[]{:S(2)}, u32[]{:S(2)}) %collective-permute-start.3) | collective-permute-done | bytes 65568 | tf_op jit(solution)/shard_map/ppermute | solution.py:212
  20.7 1.3 %collective-permute-start.4 = (bf16[2,32,256]{2,1,0:T(8,128)(2,1)S(1)}, bf16[2,32,256]{2,1,0:T(8,128)(2,1)S(1)}, u32[]{:S(2)}, u32[]{:S(2)}) collective-permute-start(bf16[2,32,256]{2,1,0:T(8,128)(2,1)S(1)} %slice.27), channel_id=1, source_target_pairs={{0,48},{2,50},{4,52},{6,54},{8,56},{10,58},{12,60},{14,62},{16,32}... | collective-permute-start | bytes 98312 | tf_op jit(solution)/shard_map/ppermute | solution.py:212
  22.0 0.7 %multiply_add_fusion = s32[2]{0:T(128)S(1)} fusion(s32[2]{0:T(128)} %constant.44.clone, s32[]{:T(128)S(6)} %axis_index.38), kind=kLoop, calls=%fused_computation.14 | loop fusion | flops 6 | bytes 20 | tf_op jit(solution)/shard_map/add | solution.py:201
  22.6 0.9 %collective-permute-done.4 = bf16[2,32,256]{2,1,0:T(8,128)(2,1)S(1)} collective-permute-done((bf16[2,32,256]{2,1,0:T(8,128)(2,1)S(1)}, bf16[2,32,256]{2,1,0:T(8,128)(2,1)S(1)}, u32[]{:S(2)}, u32[]{:S(2)}) %collective-permute-start.4) | collective-permute-done | bytes 32800 | tf_op jit(solution)/shard_map/ppermute | solution.py:212
  23.5 2.0 %collective-permute-start.5 = (bf16[2,32,256]{2,1,0:T(8,128)(2,1)S(1)}, bf16[2,32,256]{2,1,0:T(8,128)(2,1)S(1)}, u32[]{:S(2)}, u32[]{:S(2)}) collective-permute-start(bf16[2,32,256]{2,1,0:T(8,128)(2,1)S(1)} %slice_add_fusion.1.here), channel_id=1, source_target_pairs={{0,1},{1,0},{2,3},{3,2},{4,5},{5,4},{6,7},{7,6},{8,9},{9,8},{10,11... | collective-permute-start | bytes 98312 | tf_op jit(solution)/shard_map/ppermute | solution.py:231
  25.6 0.7 %stack_broadcast_in_dim.4 = s32[1,4,32]{2,1,0:T(4,128)S(1)} broadcast(s32[4]{0:T(128)} %param.23), dimensions={1} | broadcast | bytes 528 | tf_op jit(solution)/shard_map/stack;broadcast_in_dim | solution.py:198
  26.3 0.7 %stack_broadcast_in_dim.5 = s32[1,4,32]{2,1,0:T(4,128)S(1)} broadcast(s32[4]{0:T(128)} %param.24), dimensions={1} | broadcast | bytes 528 | tf_op jit(solution)/shard_map/stack;broadcast_in_dim | solution.py:198
  27.0 0.9 %fusion = s32[4]{0:T(128)S(1)} fusion(s32[1,4,32]{2,1,0:T(4,128)S(1)} %stack_broadcast_in_dim.5, s32[1,4,32]{2,1,0:T(4,128)S(1)} %stack_broadcast_in_dim.4, s32[1,4,32]{2,1,0:T(4,128)} %bitcast.12, s32[1,4,32]{2,1,0:T(4,128)} %bitcast.13, pred[4,32]{1,0:T(4,128)(4,1)S(1)} %broadcast_compare_fusion.1), kind=kLoop, calls=%fused_computation.8 | loop fusion | flops 2556 | bytes 2192 | tf_op jit(solution)/shard_map/reduce_sum | solution.py:199
  27.9 0.0 collective-permute-done.5.across
  27.9 3.8 %collective-permute-start.6 = (bf16[2,32,256]{2,1,0:T(8,128)(2,1)S(1)}, bf16[2,32,256]{2,1,0:T(8,128)(2,1)S(1)}, u32[]{:S(2)}, u32[]{:S(2)}) collective-permute-start(bf16[2,32,256]{2,1,0:T(8,128)(2,1)S(1)} %pad_maximum_fusion.3), channel_id=1, source_target_pairs={{0,65},{1,64},{64,1},{65,0},{2,67},{3,66},{66,3},{67,2},{4,69},{5,... | collective-permute-start | bytes 98312 | tf_op jit(solution)/shard_map/ppermute | solution.py:233
  31.7 0.1 pad_add_fusion.info
  31.8 0.0 copy-done.5
  31.8 0.0 copy-done.6
  31.8 0.0 copy-done.7
  31.8 0.0 copy-done.8
  31.8 0.0 copy-done.9
  31.9 1.7 %collective-permute-done.6.far = bf16[2,32,256]{2,1,0:T(8,128)(2,1)S(1)} collective-permute-done((bf16[2,32,256]{2,1,0:T(8,128)(2,1)S(1)}, bf16[2,32,256]{2,1,0:T(8,128)(2,1)S(1)}, u32[]{:S(2)}, u32[]{:S(2)}) %collective-permute-start.6) | collective-permute-done | bytes 32800 | tf_op jit(solution)/shard_map/ppermute | solution.py:233
  33.6 0.0 copy-done.2
  33.6 0.0 copy-done.1
  33.6 0.0 copy-done.3
  33.6 0.0 copy-done.4
  33.6 0.0 copy-done
  33.6 13.2 %shard_map.208 = bf16[2,100,384]{2,1,0:T(8,128)(2,1)S(1)} custom-call(s32[6]{0:T(128)S(1)} %pad_add_fusion.info, bf16[2,32,256]{2,1,0:T(8,128)(2,1)S(1)} %slice_add_fusion.1.here, bf16[2,32,256]{2,1,0:T(8,128)(2,1)S(1)} %collective-permute-done.5.across, bf16[2,32,256]{2,1,0:T(8,128)(2,1)S(1)} %collective-permute-done.6.far, f32[5,384]{1,0:T(8,128)S(1)} %stack.39.vectors, ...), custom_call_target="tpu_custom_call" | custom-call | flops 6178996224 | bytes 16777216 | tf_op jit(solution)/shard_map/pallas_call | solution.py:171
  46.8 0.8 %copy.26 = bf16[1,1,2,100,384]{4,2,3,1,0:T(2,128)(2,1)} copy(bf16[1,1,2,100,384]{4,3,2,1,0:T(8,128)(2,1)S(1)} %bitcast.5) | data formatting | bytes 307200 | tf_op jit(solution)/shard_map/broadcast_in_dim | solution.py:237
  (20 shorter events, 0.1 us)
Async XLA Ops:
  0.0 33.6 %copy-start.2 = (bf16[400,224]{1,0:T(8,128)(2,1)S(1)}, bf16[400,224]{1,0:T(8,128)(2,1)}, u32[]{:S(2)}) copy-start(bf16[400,224]{1,0:T(8,128)(2,1)} %constant.45.clone.to_one_h) | copy-start | bytes 537604
  0.0 33.6 %copy-start.1 = (bf16[512,144]{1,0:T(8,128)(2,1)S(1)}, bf16[512,144]{1,0:T(8,128)(2,1)}, u32[]{:S(2)}) copy-start(bf16[512,144]{1,0:T(8,128)(2,1)} %constant.46.clone.to_two_h) | copy-start | bytes 442372
  0.0 33.6 %copy-start.3 = (bf16[128,224]{1,0:T(8,128)(2,1)S(1)}, bf16[128,224]{1,0:T(8,128)(2,1)}, u32[]{:S(2)}) copy-start(bf16[128,224]{1,0:T(8,128)(2,1)} %constant.47.clone.to_skip_h) | copy-start | bytes 172036
  0.0 33.6 %copy-start.4 = (bf16[112,128]{1,0:T(8,128)(2,1)S(1)}, bf16[112,128]{1,0:T(8,128)(2,1)}, u32[]{:S(2)}) copy-start(bf16[112,128]{1,0:T(8,128)(2,1)} %constant.48.clone.to_out_h) | copy-start | bytes 86020
  0.0 31.8 %copy-start.5 = (f32[384]{0:T(512)S(1)}, f32[384]{0:T(512)}, u32[]{:S(2)}) copy-start(f32[384]{0:T(512)} %param.29) | copy-start | bytes 4612
  0.0 31.8 %copy-start.6 = (f32[384]{0:T(512)S(1)}, f32[384]{0:T(512)}, u32[]{:S(2)}) copy-start(f32[384]{0:T(512)} %param.30) | copy-start | bytes 4612
  0.0 31.8 %copy-start.7 = (f32[384]{0:T(512)S(1)}, f32[384]{0:T(512)}, u32[]{:S(2)}) copy-start(f32[384]{0:T(512)} %param.32) | copy-start | bytes 4612
  0.0 31.8 %copy-start.8 = (f32[384]{0:T(512)S(1)}, f32[384]{0:T(512)}, u32[]{:S(2)}) copy-start(f32[384]{0:T(512)} %param.33) | copy-start | bytes 4612
  0.0 31.8 %copy-start.9 = (f32[384]{0:T(512)S(1)}, f32[384]{0:T(512)}, u32[]{:S(2)}) copy-start(f32[384]{0:T(512)} %param.35) | copy-start | bytes 4612
  0.1 33.6 %copy-start = (bf16[432,384]{1,0:T(8,128)(2,1)S(1)}, bf16[432,384]{1,0:T(8,128)(2,1)}, u32[]{:S(2)}) copy-start(bf16[432,384]{1,0:T(8,128)(2,1)} %w_in_h.1) | copy-start | bytes 995332
  1.0 2.1 %collective-permute-start = (bf16[2,1,2,16,256]{4,3,2,1,0:T(8,128)(2,1)S(1)}, bf16[2,1,2,16,256]{4,3,2,1,0:T(8,128)(2,1)S(1)}, u32[]{:S(2)}, u32[]{:S(2)}) collective-permute-start(bf16[2,1,2,16,256]{4,3,2,1,0:T(8,128)(2,1)S(1)} %convert.14), channel_id=1, source_target_pairs={{0,2},{2,0},{4,6},{6,4},{8,10},{10,8},{12,14},{14,12},{16,18},{18,... | collective-permute-start | bytes 98312 | tf_op jit(solution)/shard_map/ppermute | solution.py:212
  3.2 4.6 %collective-permute-start.1 = (bf16[4,32,256]{2,1,0:T(8,128)(2,1)S(1)}, bf16[4,32,256]{2,1,0:T(8,128)(2,1)S(1)}, u32[]{:S(2)}, u32[]{:S(2)}) collective-permute-start(bf16[4,32,256]{2,1,0:T(8,128)(2,1)S(1)} %pad_maximum_fusion.2), channel_id=1, source_target_pairs={{0,4},{2,6},{4,0},{6,2},{8,12},{10,14},{12,8},{14,10},{16,20},{18,... | collective-permute-start | bytes 196616 | tf_op jit(solution)/shard_map/ppermute | solution.py:212
  7.7 6.4 %collective-permute-start.2 = (bf16[8,32,256]{2,1,0:T(8,128)(2,1)S(1)}, bf16[8,32,256]{2,1,0:T(8,128)(2,1)S(1)}, u32[]{:S(2)}, u32[]{:S(2)}) collective-permute-start(bf16[8,32,256]{2,1,0:T(8,128)(2,1)S(1)} %pad_maximum_fusion.1), channel_id=1, source_target_pairs={{0,12},{2,14},{4,8},{6,10},{8,4},{10,6},{12,0},{14,2},{16,28},{18,... | collective-permute-start | bytes 393224 | tf_op jit(solution)/shard_map/ppermute | solution.py:212
  14.5 6.2 %collective-permute-start.3 = (bf16[4,32,256]{2,1,0:T(8,128)(2,1)S(1)}, bf16[4,32,256]{2,1,0:T(8,128)(2,1)S(1)}, u32[]{:S(2)}, u32[]{:S(2)}) collective-permute-start(bf16[4,32,256]{2,1,0:T(8,128)(2,1)S(1)} %slice.25), channel_id=1, source_target_pairs={{0,16},{2,18},{4,20},{6,22},{8,24},{10,26},{12,28},{14,30},{16,0},... | collective-permute-start | bytes 196616 | tf_op jit(solution)/shard_map/ppermute | solution.py:212
  20.7 2.9 %collective-permute-start.4 = (bf16[2,32,256]{2,1,0:T(8,128)(2,1)S(1)}, bf16[2,32,256]{2,1,0:T(8,128)(2,1)S(1)}, u32[]{:S(2)}, u32[]{:S(2)}) collective-permute-start(bf16[2,32,256]{2,1,0:T(8,128)(2,1)S(1)} %slice.27), channel_id=1, source_target_pairs={{0,48},{2,50},{4,52},{6,54},{8,56},{10,58},{12,60},{14,62},{16,32}... | collective-permute-start | bytes 98312 | tf_op jit(solution)/shard_map/ppermute | solution.py:212
  23.5 4.3 %collective-permute-start.5 = (bf16[2,32,256]{2,1,0:T(8,128)(2,1)S(1)}, bf16[2,32,256]{2,1,0:T(8,128)(2,1)S(1)}, u32[]{:S(2)}, u32[]{:S(2)}) collective-permute-start(bf16[2,32,256]{2,1,0:T(8,128)(2,1)S(1)} %slice_add_fusion.1.here), channel_id=1, source_target_pairs={{0,1},{1,0},{2,3},{3,2},{4,5},{5,4},{6,7},{7,6},{8,9},{9,8},{10,11... | collective-permute-start | bytes 98312 | tf_op jit(solution)/shard_map/ppermute | solution.py:231
  27.9 5.7 %collective-permute-start.6 = (bf16[2,32,256]{2,1,0:T(8,128)(2,1)S(1)}, bf16[2,32,256]{2,1,0:T(8,128)(2,1)S(1)}, u32[]{:S(2)}, u32[]{:S(2)}) collective-permute-start(bf16[2,32,256]{2,1,0:T(8,128)(2,1)S(1)} %pad_maximum_fusion.3), channel_id=1, source_target_pairs={{0,65},{1,64},{64,1},{65,0},{2,67},{3,66},{66,3},{67,2},{4,69},{5,... | collective-permute-start | bytes 98312 | tf_op jit(solution)/shard_map/ppermute | solution.py:233

commit v3 on v2

--- a/solution.py
+++ b/solution.py
@@ -57,7 +57,7 @@
 
 
 def decode_kernel(
-    info, here, across, far, vectors, w_in_h, to_one_h, to_two_h, to_skip_h, to_out_h, w_one, w_two, out,
+    info, here, across, far, b_in, gain_one, b_one, gain_two, b_two, w_in_h, to_one_h, to_two_h, to_skip_h, to_out_h, w_one, w_two, out,
     w_in, to_one, to_two, to_skip, to_out, lhs, act_one, act_two, skip, middle, w_one_v, w_two_v, small, sems,
 ):
     tables = []
@@ -77,7 +77,9 @@
             copies.append(copy)
     row0, col0, high, count, section = info[0], info[1], (2 + 2 * info[2]) * TS - 3, info[3], info[4]
     wide, first = info[5], 2 * section - 2
-    b_in, gain_one, b_one, gain_two, b_two = [vectors[n : n + 1, :] for n in range(5)]
+    b_in, gain_one, b_one, gain_two, b_two = [
+        v[...].reshape(1, CH) for v in (b_in, gain_one, b_one, gain_two, b_two)
+    ]
 
     lane = lax.broadcasted_iota(jnp.int32, (SPAN * EXT, EXT * ZC), 1)
     line = lax.broadcasted_iota(jnp.int32, (SPAN * EXT, EXT * ZC), 0)
@@ -171,7 +173,7 @@
     return pl.pallas_call(
         decode_kernel,
         out_shape=jax.ShapeDtypeStruct((2, TS * TS, CH), BF16),
-        in_specs=[pl.BlockSpec(memory_space=pltpu.SMEM)] + [vmem] * 4 + [hbm] * 7,
+        in_specs=[pl.BlockSpec(memory_space=pltpu.SMEM)] + [vmem] * 8 + [hbm] * 7,
         out_specs=vmem,
         scratch_shapes=[pltpu.VMEM(t.shape, BF16) for t in tables]
         + [
@@ -189,17 +191,28 @@
         cost_estimate=pl.CostEstimate(
             flops=2 * 27 * CH * CH * (SPAN * MID_ROWS + 200), bytes_accessed=16 << 20, transcendentals=0
         ),
-    )(info, here, across, far, vectors, *tables, w_one, w_two)
-
-
-def slot_info(resolution, frame_counts, tile_rows, tile_cols, decoder_list, mine):
-    match = decoder_list == mine
-    wide = lambda t: jnp.broadcast_to(t[:, None], match.shape)
-    tables = jnp.stack([tile_rows, tile_cols, wide(resolution), wide(frame_counts)])
-    picked = jnp.sum(jnp.where(match[None], tables, 0), axis=(1, 2))
-    place = jnp.array([0, lax.axis_size("tile") // 4 * TS - 4], jnp.int32)
-    place = place + jnp.array([1, 0], jnp.int32) * lax.axis_index("section")
-    return jnp.concatenate([picked, place]).astype(jnp.int32)
+    )(info, here, across, far, *vectors, *tables, w_one, w_two)
+
+
+def iota(shape, dim):
+    return lax.broadcasted_iota(jnp.int32, shape, dim)
+
+
+def slot_info(resolution, frame_counts, tile_rows, tile_cols, decoder_list, mine, width):
+    shape = (6,) + decoder_list.shape
+    which = iota(shape, 0)
+    table = jnp.where(
+        which == 0,
+        tile_rows[None],
+        jnp.where(
+            which == 1,
+            tile_cols[None],
+            jnp.where(which == 2, resolution[None, :, None], frame_counts[None, :, None]),
+        ),
+    )
+    picked = jnp.sum(jnp.where((decoder_list == mine)[None] & (which < 4), table, 0), axis=(1, 2))
+    place = iota((6,), 0)
+    return picked + jnp.where(place == 4, lax.axis_index("section"), jnp.where(place == 5, width, 0))
 
 
 def local(
@@ -209,31 +222,40 @@
     tiles = lax.axis_size("tile")
     video, tile = lax.axis_index("video"), lax.axis_index("tile")
     mine = video * tiles + tile
-    flip = lambda a, by, count=tiles: lax.ppermute(a, "tile", [(i, i ^ by) for i in range(count)])
+    flip = lambda a, by: lax.ppermute(a, "tile", [(i, i ^ by) for i in range(tiles)])
     unit = (2 * EXT, EXT * ZC)
-
-    first = flip(latent, 1)
-    have = jnp.concatenate([latent, first]).astype(BF16).reshape(4, *unit)
-    have = jnp.concatenate([have, flip(have, 2)])
+    after = lambda done, *args: lax.optimization_barrier((done, *args))
+
+    live = (tile < tiles // 2).astype(F32)
+    first = flip(latent, 2) * live
+    have = jnp.concatenate([latent.astype(BF16), first.astype(BF16)]).reshape(4, *unit)
     have = jnp.concatenate([have, flip(have, 6)])
-    hops = np.array([far ^ near ^ core for far in (0, 6) for near in (0, 2) for core in (0, 1)], np.int32)
-    slots = (tile ^ hops)[:, None] == jnp.arange(tiles, dtype=jnp.int32)
-    names = lax.dynamic_slice(decoder_list, (2 * video, 0), (2, tiles))
-    names = jnp.sum(jnp.where(slots[:, None], names[None], 0), axis=-1).reshape(16)
-
-    rows = np.array([row ^ group for row in (0, 24, 8, 16) for group in (0, tiles)], np.int32)
-    match = (mine ^ rows)[:, None] == names[None, :]
+    have = jnp.concatenate([have, flip(have, 1)])
+
+    shape = (8, 2) + decoder_list.shape
+    step = iota(shape, 0)
+    hop = (step >> 2) ^ ((step >> 1) & 1) * 6 ^ (step & 1) * 2
+    here = (iota(shape, 2) == 2 * video + iota(shape, 1)) & (iota(shape, 3) == tile ^ hop)
+    names = jnp.sum(jnp.where(here, decoder_list, 0), axis=(2, 3))
+
+    shape = (8, 8, 2)
+    row = iota(shape, 0)
+    goal = mine ^ (row & 1) * tiles ^ ((row >> 1) & 1) * 24 ^ (row >> 2) * 8
+    match = (goal == names[None]).reshape(8, 16)
     kept = jnp.sum(
         jnp.where(match[:, :, None, None], have[None], jnp.zeros((), BF16)), axis=1, dtype=F32
     ).astype(BF16)
-    kept = kept[:4] + flip(kept[4:], 8, 16)
-    here = kept[:2] + flip(kept[2:], 24, 16)
+    kept = kept[:4] + flip(kept[4:], 8)
+    here = kept[:2] + flip(kept[2:], 24)
     across = lax.ppermute(here, "section", [(0, 1), (1, 0)])
     outward = jnp.stack([here[1], across[1]])
     far = lax.ppermute(outward, ("video", "section"), [(z, z ^ 3) for z in range(4)])
 
-    info = slot_info(resolution, frame_counts, tile_rows, tile_cols, decoder_list, mine)
-    vectors = jnp.stack([b_in, gain_one, b_one, gain_two, b_two])
+    _, resolution, frame_counts = after(kept, resolution, frame_counts)
+    info = slot_info(
+        resolution, frame_counts, tile_rows, tile_cols, decoder_list, mine, tiles // 4 * TS - 4
+    )
+    vectors = [b_in, gain_one, b_one, gain_two, b_two]
     return decode(info, here, across, far, vectors, w_in, w_one, w_two)[None, None]
 
 

time: 48.5 us -> 46 us (0.948); the launches traced: 47.6 us -> 45.8 us
  local copies, waits for them, and re-layouts: 3.18 us -> 1 us
  other arithmetic: 5.22 us -> 3.9 us
  waiting for transfers between devices: 10.5 us -> 11.5 us
  starting transfers between devices: 15.3 us -> 16.1 us
    another operation x8 -> x0, local copies, waits for them, and re-layouts: 1.49 us -> none  [the longest x2 1.45 us: slot_info(): jnp.stack([tile_rows, tile_cols, wide(resolution), wide(frame_counts)])]
    xor x2, other arithmetic: 1.32 us -> 0.02 us  [the longest x1 0.01 us: local(): tile ^ hop]
    another operation x1 -> x0, other arithmetic: 0.98 us -> none
    convert_element_type x0 -> x2, other arithmetic: none -> 0.89 us  [the longest x1 0.88 us: local(): latent.astype(BF16)]
    ppermute x1, waiting for transfers between devices: 0.01 us -> 0.88 us  [local(): across = lax.ppermute(here, 'section', [(0, 1), (1, 0)])]
    reduce_sum x2, other arithmetic: 1 us -> 1.87 us  [the longest x1 1 us: slot_info(): jnp.sum(jnp.where((decoder_list == mine)[None] & (which < 4), table, 0),...]
    dynamic_slice x1 -> x0, local copies, waits for them, and re-layouts: 0.69 us -> none  [local(): names = lax.dynamic_slice(decoder_list, (2 * video, 0), (2, tiles))]
    add x3 -> x4, other arithmetic: 0.68 us -> 0.02 us  [the longest x1 0.01 us: local(): kept = kept[:4] + flip(kept[4:], 8)]
  transfers between devices with their start and end apart: 7 -> 7, of which waited for: 5 -> 7; matrix products, arithmetic and copies ran while one was open for 13% -> 8% of each run, Pallas kernels for 0% -> 0%
where the time goes in v3:
time: 46 us; the launch traced here: 45.8 us
  starting transfers between devices  16.1 us (35%)
  Pallas kernels  13.2 us (29%)
  waiting for transfers between devices  11.5 us (25%)
  other arithmetic  3.9 us (8%)
  local copies, waits for them, and re-layouts  1 us (2%)
    pallas_call x1, Pallas kernels, decode(): pl.pallas_call(decode_kernel, out_shape=jax.ShapeDtypeStruct((2, TS * TS,...  13.2 us
    ppermute x5, starting transfers between devices, local(): lax.ppermute(a, 'tile', [(i, i ^ by) for i in range(tiles)])  9.65 us
    ppermute x5, waiting for transfers between devices, local(): lax.ppermute(a, 'tile', [(i, i ^ by) for i in range(tiles)])  8.7 us
    ppermute x1, starting transfers between devices, local(): lax.ppermute(outward, ('video', 'section'), [(z, z ^ 3) for z in range(4)])  4.4 us
    ppermute x1, starting transfers between devices, local(): across = lax.ppermute(here, 'section', [(0, 1), (1, 0)])  2.02 us
    ppermute x1, waiting for transfers between devices, local(): lax.ppermute(outward, ('video', 'section'), [(z, z ^ 3) for z in range(4)])  1.89 us
    reduce_sum x1, other arithmetic, slot_info(): jnp.sum(jnp.where((decoder_list == mine)[None] & (which < 4), table, 0),...  1 us
  transfers between devices with their start and end apart: 7, of which 7 were waited for; matrix products, arithmetic and copies ran while one was open for 8% of the time, Pallas kernels for 0%

profile of v3, /device:TPU:0, one launch (start us, length us, event | category | flops | bytes accessed | tf_op | source)
XLA Modules:
  0.0 45.8 jit_solution(16975187794804161637)
XLA Ops:
  0.0 0.0 copy-start.7
  0.0 0.0 copy-start.6
  0.0 0.0 copy-start.8
  0.0 0.0 copy-start.9
  0.0 0.0 copy-start
  0.0 0.0 copy-start.1
  0.0 0.0 copy-start.2
  0.0 0.0 copy-start.3
  0.0 0.0 copy-start.4
  0.1 0.0 copy-start.5
  0.1 1.7 %collective-permute-start = (f32[2,1,2,16,256]{4,3,2,1,0:T(8,128)}, f32[2,1,2,16,256]{4,3,2,1,0:T(8,128)S(1)}, u32[]{:S(2)}, u32[]{:S(2)}) collective-permute-start(f32[2,1,2,16,256]{4,3,2,1,0:T(8,128)} %param.18), channel_id=1, source_target_pairs={{0,4},{2,6},{4,0},{6,2},{8,12},{10,14},{12,8},{14,10},{16,20},{18,... | collective-permute-start | bytes 196616 | tf_op jit(solution)/shard_map/ppermute | solution.py:225
  1.7 0.9 %convert_element_type.11 = bf16[2,1,2,16,256]{4,3,2,1,0:T(8,128)(2,1)S(1)} convert(f32[2,1,2,16,256]{4,3,2,1,0:T(8,128)} %param.18) | non-fusion elementwise | flops 16384 | bytes 98304 | tf_op jit(solution)/shard_map/convert_element_type | solution.py:231
  2.6 0.7 %broadcast_compare_fusion.1 = pred[4,32]{1,0:T(4,128)(4,1)S(1)} fusion(s32[4,32]{1,0:T(4,128)} %param.23, s32[]{:T(128)S(6)} %add.19), kind=kLoop, calls=%fused_computation.16 | loop fusion | flops 128 | bytes 644 | tf_op jit(solution)/shard_map/eq | solution.py:213
  3.3 0.9 %select_reduce_fusion.1 = s32[8,2]{0,1:T(2,128)S(1)} fusion(s32[4,32]{1,0:T(4,128)} %param.23, s32[8]{0:T(128)S(1)} %xor_xor_fusion, s32[2]{0:T(128)S(1)} %iota_add_fusion), kind=kLoop, calls=%fused_computation.8 | loop fusion | flops 10224 | bytes 616 | tf_op jit(solution)/shard_map/reduce_sum | solution.py:239
  4.2 0.1 copy.21
  4.3 0.1 eq.65
  4.4 0.2 collective-permute-done
  4.6 2.9 %collective-permute-start.1 = (bf16[4,32,256]{2,1,0:T(8,128)(2,1)S(1)}, bf16[4,32,256]{2,1,0:T(8,128)(2,1)S(1)}, u32[]{:S(2)}, u32[]{:S(2)}) collective-permute-start(bf16[4,32,256]{2,1,0:T(8,128)(2,1)S(1)} %bitcast.3), channel_id=1, source_target_pairs={{0,12},{2,14},{4,8},{6,10},{8,4},{10,6},{12,0},{14,2},{16,28},{18,... | collective-permute-start | bytes 196616 | tf_op jit(solution)/shard_map/ppermute | solution.py:225
  7.6 2.6 %collective-permute-done.1 = bf16[4,32,256]{2,1,0:T(8,128)(2,1)S(1)} collective-permute-done((bf16[4,32,256]{2,1,0:T(8,128)(2,1)S(1)}, bf16[4,32,256]{2,1,0:T(8,128)(2,1)S(1)}, u32[]{:S(2)}, u32[]{:S(2)}) %collective-permute-start.1) | collective-permute-done | bytes 65568 | tf_op jit(solution)/shard_map/ppermute | solution.py:225
  10.2 0.1 collective-permute-start.2
  10.3 0.1 broadcast_compare_fusion
  10.4 1.3 %collective-permute-done.2 = bf16[8,32,256]{2,1,0:T(8,128)(2,1)S(1)} collective-permute-done((bf16[8,32,256]{2,1,0:T(8,128)(2,1)S(1)}, bf16[8,32,256]{2,1,0:T(8,128)(2,1)S(1)}, u32[]{:S(2)}, u32[]{:S(2)}) %collective-permute-start.2) | collective-permute-done | bytes 131104 | tf_op jit(solution)/shard_map/ppermute | solution.py:225
  11.7 0.3 select_reduce_fusion
  12.0 1.8 %collective-permute-start.3 = (bf16[4,32,256]{2,1,0:T(8,128)(2,1)S(1)}, bf16[4,32,256]{2,1,0:T(8,128)(2,1)S(1)}, u32[]{:S(2)}, u32[]{:S(2)}) collective-permute-start(bf16[4,32,256]{2,1,0:T(8,128)(2,1)S(1)} %slice.25), channel_id=1, source_target_pairs={{0,16},{2,18},{4,20},{6,22},{8,24},{10,26},{12,28},{14,30},{16,0},... | collective-permute-start | bytes 196616 | tf_op jit(solution)/shard_map/ppermute | solution.py:225
  13.7 2.6 %collective-permute-done.3 = bf16[4,32,256]{2,1,0:T(8,128)(2,1)S(1)} collective-permute-done((bf16[4,32,256]{2,1,0:T(8,128)(2,1)S(1)}, bf16[4,32,256]{2,1,0:T(8,128)(2,1)S(1)}, u32[]{:S(2)}, u32[]{:S(2)}) %collective-permute-start.3) | collective-permute-done | bytes 65568 | tf_op jit(solution)/shard_map/ppermute | solution.py:225
  16.3 3.2 %collective-permute-start.4 = (bf16[2,32,256]{2,1,0:T(8,128)(2,1)S(1)}, bf16[2,32,256]{2,1,0:T(8,128)(2,1)S(1)}, u32[]{:S(2)}, u32[]{:S(2)}) collective-permute-start(bf16[2,32,256]{2,1,0:T(8,128)(2,1)S(1)} %slice.27), channel_id=1, source_target_pairs={{0,48},{2,50},{4,52},{6,54},{8,56},{10,58},{12,60},{14,62},{16,32}... | collective-permute-start | bytes 98312 | tf_op jit(solution)/shard_map/ppermute | solution.py:225
  19.5 2.0 %collective-permute-done.4 = bf16[2,32,256]{2,1,0:T(8,128)(2,1)S(1)} collective-permute-done((bf16[2,32,256]{2,1,0:T(8,128)(2,1)S(1)}, bf16[2,32,256]{2,1,0:T(8,128)(2,1)S(1)}, u32[]{:S(2)}, u32[]{:S(2)}) %collective-permute-start.4) | collective-permute-done | bytes 32800 | tf_op jit(solution)/shard_map/ppermute | solution.py:225
  21.6 2.0 %collective-permute-start.5 = (bf16[2,32,256]{2,1,0:T(8,128)(2,1)S(1)}, bf16[2,32,256]{2,1,0:T(8,128)(2,1)S(1)}, u32[]{:S(2)}, u32[]{:S(2)}) collective-permute-start(bf16[2,32,256]{2,1,0:T(8,128)(2,1)S(1)} %slice_add_fusion.1.here), channel_id=1, source_target_pairs={{0,1},{1,0},{2,3},{3,2},{4,5},{5,4},{6,7},{7,6},{8,9},{9,8},{10,11... | collective-permute-start | bytes 98312 | tf_op jit(solution)/shard_map/ppermute | solution.py:250
  23.6 1.0 %select_reduce_fusion.2 = s32[6]{0:T(128)S(1)} fusion(s32[4]{0:T(128)} %param.20, s32[4]{0:T(128)} %param.19, s32[4,32]{1,0:T(4,128)} %param.22, s32[4,32]{1,0:T(4,128)} %param.21, pred[6]{0:T(512)(128)(4,1)S(1)} %get-tuple-element.9, pred[6]{0:T(512)(128)(4,1)S(1)} %get-tuple-element.10, pred[6]{0:T(512)(128)(4,1)S(1)} %get-tuple-element.11, ...), kind=kLoop, calls=%fused_computation.12 | loop fusion | flops 4602 | bytes 1232 | tf_op jit(solution)/shard_map/reduce_sum | solution.py:213
  24.6 0.9 %collective-permute-done.5.across = bf16[2,32,256]{2,1,0:T(8,128)(2,1)S(1)} collective-permute-done((bf16[2,32,256]{2,1,0:T(8,128)(2,1)S(1)}, bf16[2,32,256]{2,1,0:T(8,128)(2,1)S(1)}, u32[]{:S(2)}, u32[]{:S(2)}) %collective-permute-start.5) | collective-permute-done | bytes 32800 | tf_op jit(solution)/shard_map/ppermute | solution.py:250
  25.5 4.4 %collective-permute-start.6 = (bf16[2,32,256]{2,1,0:T(8,128)(2,1)S(1)}, bf16[2,32,256]{2,1,0:T(8,128)(2,1)S(1)}, u32[]{:S(2)}, u32[]{:S(2)}) collective-permute-start(bf16[2,32,256]{2,1,0:T(8,128)(2,1)S(1)} %pad_maximum_fusion.3), channel_id=1, source_target_pairs={{0,65},{1,64},{64,1},{65,0},{2,67},{3,66},{66,3},{67,2},{4,69},{5,... | collective-permute-start | bytes 98312 | tf_op jit(solution)/shard_map/ppermute | solution.py:252
  29.9 1.9 %collective-permute-done.6.far = bf16[2,32,256]{2,1,0:T(8,128)(2,1)S(1)} collective-permute-done((bf16[2,32,256]{2,1,0:T(8,128)(2,1)S(1)}, bf16[2,32,256]{2,1,0:T(8,128)(2,1)S(1)}, u32[]{:S(2)}, u32[]{:S(2)}) %collective-permute-start.6) | collective-permute-done | bytes 32800 | tf_op jit(solution)/shard_map/ppermute | solution.py:252
  31.8 0.0 copy-done.7
  31.8 0.0 copy-done.6
  31.8 0.0 copy-done.8
  31.8 0.0 copy-done.9
  31.8 0.0 copy-done
  31.8 0.0 copy-done.1
  31.8 0.0 copy-done.2
  31.8 0.0 copy-done.3
  31.8 0.0 copy-done.4
  31.8 0.0 copy-done.5
  31.9 13.2 %shard_map.172 = bf16[2,100,384]{2,1,0:T(8,128)(2,1)S(1)} custom-call(s32[6]{0:T(128)S(1)} %fusion.1.info, bf16[2,32,256]{2,1,0:T(8,128)(2,1)S(1)} %slice_add_fusion.1.here, bf16[2,32,256]{2,1,0:T(8,128)(2,1)S(1)} %collective-permute-done.5.across, bf16[2,32,256]{2,1,0:T(8,128)(2,1)S(1)} %collective-permute-done.6.far, f32[384]{0:T(512)S(1)} %copy-done.1, ...), custom_call_target="tpu_custom_call" | custom-call | flops 6178996224 | bytes 16777216 | tf_op jit(solution)/shard_map/pallas_call | solution.py:173
  45.0 0.8 %copy.22 = bf16[1,1,2,100,384]{4,2,3,1,0:T(2,128)(2,1)} copy(bf16[1,1,2,100,384]{4,3,2,1,0:T(8,128)(2,1)S(1)} %bitcast.2) | data formatting | bytes 307200 | tf_op jit(solution)/shard_map/broadcast_in_dim | solution.py:259
  (17 shorter events, 0.1 us)
Async XLA Ops:
  0.0 31.8 %copy-start.7 = (bf16[400,224]{1,0:T(8,128)(2,1)S(1)}, bf16[400,224]{1,0:T(8,128)(2,1)}, u32[]{:S(2)}) copy-start(bf16[400,224]{1,0:T(8,128)(2,1)} %constant.15.clone.to_one_h) | copy-start | bytes 537604
  0.0 31.8 %copy-start.6 = (bf16[512,144]{1,0:T(8,128)(2,1)S(1)}, bf16[512,144]{1,0:T(8,128)(2,1)}, u32[]{:S(2)}) copy-start(bf16[512,144]{1,0:T(8,128)(2,1)} %constant.16.clone.to_two_h) | copy-start | bytes 442372
  0.0 31.8 %copy-start.8 = (bf16[128,224]{1,0:T(8,128)(2,1)S(1)}, bf16[128,224]{1,0:T(8,128)(2,1)}, u32[]{:S(2)}) copy-start(bf16[128,224]{1,0:T(8,128)(2,1)} %constant.17.clone.to_skip_h) | copy-start | bytes 172036
  0.0 31.8 %copy-start.9 = (bf16[112,128]{1,0:T(8,128)(2,1)S(1)}, bf16[112,128]{1,0:T(8,128)(2,1)}, u32[]{:S(2)}) copy-start(bf16[112,128]{1,0:T(8,128)(2,1)} %constant.18.clone.to_out_h) | copy-start | bytes 86020
  0.0 31.8 %copy-start = (bf16[432,384]{1,0:T(8,128)(2,1)S(1)}, bf16[432,384]{1,0:T(8,128)(2,1)}, u32[]{:S(2)}) copy-start(bf16[432,384]{1,0:T(8,128)(2,1)} %w_in_h.1) | copy-start | bytes 995332
  0.0 31.8 %copy-start.1 = (f32[384]{0:T(512)S(1)}, f32[384]{0:T(512)}, u32[]{:S(2)}) copy-start(f32[384]{0:T(512)} %b_in.1) | copy-start | bytes 4612
  0.0 31.8 %copy-start.2 = (f32[384]{0:T(512)S(1)}, f32[384]{0:T(512)}, u32[]{:S(2)}) copy-start(f32[384]{0:T(512)} %gain_one.1) | copy-start | bytes 4612
  0.0 31.8 %copy-start.3 = (f32[384]{0:T(512)S(1)}, f32[384]{0:T(512)}, u32[]{:S(2)}) copy-start(f32[384]{0:T(512)} %b_one.1) | copy-start | bytes 4612
  0.0 31.8 %copy-start.4 = (f32[384]{0:T(512)S(1)}, f32[384]{0:T(512)}, u32[]{:S(2)}) copy-start(f32[384]{0:T(512)} %gain_two.1) | copy-start | bytes 4612
  0.1 31.8 %copy-start.5 = (f32[384]{0:T(512)S(1)}, f32[384]{0:T(512)}, u32[]{:S(2)}) copy-start(f32[384]{0:T(512)} %b_two.1) | copy-start | bytes 4612
  0.1 4.6 %collective-permute-start = (f32[2,1,2,16,256]{4,3,2,1,0:T(8,128)}, f32[2,1,2,16,256]{4,3,2,1,0:T(8,128)S(1)}, u32[]{:S(2)}, u32[]{:S(2)}) collective-permute-start(f32[2,1,2,16,256]{4,3,2,1,0:T(8,128)} %param.18), channel_id=1, source_target_pairs={{0,4},{2,6},{4,0},{6,2},{8,12},{10,14},{12,8},{14,10},{16,20},{18,... | collective-permute-start | bytes 196616 | tf_op jit(solution)/shard_map/ppermute | solution.py:225
  4.6 5.6 %collective-permute-start.1 = (bf16[4,32,256]{2,1,0:T(8,128)(2,1)S(1)}, bf16[4,32,256]{2,1,0:T(8,128)(2,1)S(1)}, u32[]{:S(2)}, u32[]{:S(2)}) collective-permute-start(bf16[4,32,256]{2,1,0:T(8,128)(2,1)S(1)} %bitcast.3), channel_id=1, source_target_pairs={{0,12},{2,14},{4,8},{6,10},{8,4},{10,6},{12,0},{14,2},{16,28},{18,... | collective-permute-start | bytes 196616 | tf_op jit(solution)/shard_map/ppermute | solution.py:225
  10.2 1.4 %collective-permute-start.2 = (bf16[8,32,256]{2,1,0:T(8,128)(2,1)S(1)}, bf16[8,32,256]{2,1,0:T(8,128)(2,1)S(1)}, u32[]{:S(2)}, u32[]{:S(2)}) collective-permute-start(bf16[8,32,256]{2,1,0:T(8,128)(2,1)S(1)} %pad_maximum_fusion.1), channel_id=1, source_target_pairs={{0,2},{2,0},{4,6},{6,4},{8,10},{10,8},{12,14},{14,12},{16,18},{18,... | collective-permute-start | bytes 393224 | tf_op jit(solution)/shard_map/ppermute | solution.py:225
  12.0 4.3 %collective-permute-start.3 = (bf16[4,32,256]{2,1,0:T(8,128)(2,1)S(1)}, bf16[4,32,256]{2,1,0:T(8,128)(2,1)S(1)}, u32[]{:S(2)}, u32[]{:S(2)}) collective-permute-start(bf16[4,32,256]{2,1,0:T(8,128)(2,1)S(1)} %slice.25), channel_id=1, source_target_pairs={{0,16},{2,18},{4,20},{6,22},{8,24},{10,26},{12,28},{14,30},{16,0},... | collective-permute-start | bytes 196616 | tf_op jit(solution)/shard_map/ppermute | solution.py:225
  16.3 5.2 %collective-permute-start.4 = (bf16[2,32,256]{2,1,0:T(8,128)(2,1)S(1)}, bf16[2,32,256]{2,1,0:T(8,128)(2,1)S(1)}, u32[]{:S(2)}, u32[]{:S(2)}) collective-permute-start(bf16[2,32,256]{2,1,0:T(8,128)(2,1)S(1)} %slice.27), channel_id=1, source_target_pairs={{0,48},{2,50},{4,52},{6,54},{8,56},{10,58},{12,60},{14,62},{16,32}... | collective-permute-start | bytes 98312 | tf_op jit(solution)/shard_map/ppermute | solution.py:225
  21.6 3.9 %collective-permute-start.5 = (bf16[2,32,256]{2,1,0:T(8,128)(2,1)S(1)}, bf16[2,32,256]{2,1,0:T(8,128)(2,1)S(1)}, u32[]{:S(2)}, u32[]{:S(2)}) collective-permute-start(bf16[2,32,256]{2,1,0:T(8,128)(2,1)S(1)} %slice_add_fusion.1.here), channel_id=1, source_target_pairs={{0,1},{1,0},{2,3},{3,2},{4,5},{5,4},{6,7},{7,6},{8,9},{9,8},{10,11... | collective-permute-start | bytes 98312 | tf_op jit(solution)/shard_map/ppermute | solution.py:250
  25.5 6.3 %collective-permute-start.6 = (bf16[2,32,256]{2,1,0:T(8,128)(2,1)S(1)}, bf16[2,32,256]{2,1,0:T(8,128)(2,1)S(1)}, u32[]{:S(2)}, u32[]{:S(2)}) collective-permute-start(bf16[2,32,256]{2,1,0:T(8,128)(2,1)S(1)} %pad_maximum_fusion.3), channel_id=1, source_target_pairs={{0,65},{1,64},{64,1},{65,0},{2,67},{3,66},{66,3},{67,2},{4,69},{5,... | collective-permute-start | bytes 98312 | tf_op jit(solution)/shard_map/ppermute | solution.py:252

commit v4 on v3

--- a/solution.py
+++ b/solution.py
@@ -102,21 +102,32 @@
         table.wait()
     pos = lax.broadcasted_iota(jnp.int32, (STEM_ROWS, 1), 0)
     mask_one = inside(row0 - 2 + (pos & (EXT - 1)), col0 - 2 + (pos >> 4), high, wide)
+    rows = lhs[...].reshape(SPAN * STEM_ROWS, EXT * ZC)[:, : 9 * ZC]
+    part = [
+        dot(rows[: (2 + dt) * STEM_ROWS], w_in[pl.ds(dt * 9 * ZC, 9 * ZC), :]) for dt in range(3)
+    ]
+    acts, skips = [], []
     for f in range(SPAN):
         stem = b_in
         for dt in range(3):
             if f + dt - 2 >= 0:
-                left = lhs[f + dt - 2].reshape(STEM_ROWS, EXT * ZC)[:, : 9 * ZC]
-                stem = stem + dot(left, w_in[pl.ds(dt * 9 * ZC, 9 * ZC), :])
+                at = (f + dt - 2) * STEM_ROWS
+                stem = stem + part[dt][at : at + STEM_ROWS]
         act = activate(stem, gain_one) * mask_one
         if f < 2:
             act = act * (first + f >= 0).astype(F32)
-        moved = dot(to_one[...], act.astype(BF16))
-        act_one[f] = moved.astype(BF16).reshape(5, 5, 16, CH)
-        if f >= 2:
+        else:
             coarse = stem.astype(BF16)
             fine = (stem - coarse.astype(F32)).astype(BF16)
-            skip[f - 2] = dot(to_skip[...], coarse) + dot(to_skip[...], fine) + b_two
+            skips.append(jnp.concatenate([coarse, fine], axis=0))
+        acts.append(act.astype(BF16))
+    moved = dot(to_one[...], jnp.concatenate(acts, axis=1)).astype(BF16)
+    for f in range(SPAN):
+        act_one[f] = moved[:, f * CH : (f + 1) * CH].reshape(5, 5, 16, CH)
+    twice = jnp.concatenate([to_skip[...], to_skip[...]], axis=1)
+    moved = dot(twice, jnp.concatenate(skips, axis=1))
+    for f in range(2):
+        skip[f] = moved[:, f * CH : (f + 1) * CH] + b_two
 
     for step in range(3):
         dt = 2 - step
@@ -229,6 +240,7 @@
     live = (tile < tiles // 2).astype(F32)
     first = flip(latent, 2) * live
     have = jnp.concatenate([latent.astype(BF16), first.astype(BF16)]).reshape(4, *unit)
+    have, named_by = after(have, decoder_list)
     have = jnp.concatenate([have, flip(have, 6)])
     have = jnp.concatenate([have, flip(have, 1)])
 
@@ -236,7 +248,7 @@
     step = iota(shape, 0)
     hop = (step >> 2) ^ ((step >> 1) & 1) * 6 ^ (step & 1) * 2
     here = (iota(shape, 2) == 2 * video + iota(shape, 1)) & (iota(shape, 3) == tile ^ hop)
-    names = jnp.sum(jnp.where(here, decoder_list, 0), axis=(2, 3))
+    names = jnp.sum(jnp.where(here, named_by, 0), axis=(2, 3))
 
     shape = (8, 8, 2)
     row = iota(shape, 0)

time: 46 us -> 44.9 us (0.976)
  Pallas kernels: 13.2 us -> 12.3 us
    pallas_call x1, Pallas kernels: 13.2 us -> 12.3 us  [decode(): pl.pallas_call(decode_kernel, out_shape=jax.ShapeDtypeStruct((2, TS * TS,...]
where the time goes in v4:
time: 44.9 us; the launch traced here: 44.7 us
  starting transfers between devices  15.9 us (35%)
  Pallas kernels  12.3 us (27%)
  waiting for transfers between devices  11.5 us (26%)
  other arithmetic  3.9 us (9%)
  local copies, waits for them, and re-layouts  1 us (2%)
    pallas_call x1, Pallas kernels, decode(): pl.pallas_call(decode_kernel, out_shape=jax.ShapeDtypeStruct((2, TS * TS,...  12.3 us
    ppermute x5, starting transfers between devices, local(): lax.ppermute(a, 'tile', [(i, i ^ by) for i in range(tiles)])  9.65 us
    ppermute x5, waiting for transfers between devices, local(): lax.ppermute(a, 'tile', [(i, i ^ by) for i in range(tiles)])  8.7 us
    ppermute x1, starting transfers between devices, local(): lax.ppermute(outward, ('video', 'section'), [(z, z ^ 3) for z in range(4)])  4.22 us
    ppermute x1, starting transfers between devices, local(): across = lax.ppermute(here, 'section', [(0, 1), (1, 0)])  2.02 us
    ppermute x1, waiting for transfers between devices, local(): lax.ppermute(outward, ('video', 'section'), [(z, z ^ 3) for z in range(4)])  1.89 us
    reduce_sum x1, other arithmetic, slot_info(): jnp.sum(jnp.where((decoder_list == mine)[None] & (which < 4), table, 0),...  1 us
  transfers between devices with their start and end apart: 7, of which 7 were waited for; matrix products, arithmetic and copies ran while one was open for 8% of the time, Pallas kernels for 0%

profile of v4, /device:TPU:0, one launch (start us, length us, event | category | flops | bytes accessed | tf_op | source)
XLA Modules:
  0.0 44.7 jit_solution(96402667205119745)
XLA Ops:
  0.0 0.0 copy-start.7
  0.0 0.0 copy-start.6
  0.0 0.0 copy-start.8
  0.0 0.0 copy-start.9
  0.0 0.0 copy-start
  0.0 0.0 copy-start.1
  0.0 0.0 copy-start.2
  0.0 0.0 copy-start.3
  0.0 0.0 copy-start.4
  0.1 0.0 copy-start.5
  0.1 1.7 %collective-permute-start = (f32[2,1,2,16,256]{4,3,2,1,0:T(8,128)}, f32[2,1,2,16,256]{4,3,2,1,0:T(8,128)S(1)}, u32[]{:S(2)}, u32[]{:S(2)}) collective-permute-start(f32[2,1,2,16,256]{4,3,2,1,0:T(8,128)} %param.18), channel_id=1, source_target_pairs={{0,4},{2,6},{4,0},{6,2},{8,12},{10,14},{12,8},{14,10},{16,20},{18,... | collective-permute-start | bytes 196616 | tf_op jit(solution)/shard_map/ppermute | solution.py:236
  1.7 0.9 %convert_element_type.11 = bf16[2,1,2,16,256]{4,3,2,1,0:T(8,128)(2,1)S(1)} convert(f32[2,1,2,16,256]{4,3,2,1,0:T(8,128)} %param.18) | non-fusion elementwise | flops 16384 | bytes 98304 | tf_op jit(solution)/shard_map/convert_element_type | solution.py:242
  2.6 0.7 %broadcast_compare_fusion.1 = pred[4,32]{1,0:T(4,128)(4,1)S(1)} fusion(s32[4,32]{1,0:T(4,128)} %param.23, s32[]{:T(128)S(6)} %add.19), kind=kLoop, calls=%fused_computation.16 | loop fusion | flops 128 | bytes 644 | tf_op jit(solution)/shard_map/eq | solution.py:224
  3.3 1.3 %collective-permute-done = f32[2,1,2,16,256]{4,3,2,1,0:T(8,128)S(1)} collective-permute-done((f32[2,1,2,16,256]{4,3,2,1,0:T(8,128)}, f32[2,1,2,16,256]{4,3,2,1,0:T(8,128)S(1)}, u32[]{:S(2)}, u32[]{:S(2)}) %collective-permute-start) | collective-permute-done | bytes 65568 | tf_op jit(solution)/shard_map/ppermute | solution.py:236
  4.6 2.9 %collective-permute-start.1 = (bf16[4,32,256]{2,1,0:T(8,128)(2,1)S(1)}, bf16[4,32,256]{2,1,0:T(8,128)(2,1)S(1)}, u32[]{:S(2)}, u32[]{:S(2)}) collective-permute-start(bf16[4,32,256]{2,1,0:T(8,128)(2,1)S(1)} %bitcast.3), channel_id=1, source_target_pairs={{0,12},{2,14},{4,8},{6,10},{8,4},{10,6},{12,0},{14,2},{16,28},{18,... | collective-permute-start | bytes 196616 | tf_op jit(solution)/shard_map/ppermute | solution.py:236
  7.6 0.9 %select_reduce_fusion.1 = s32[8,2]{0,1:T(2,128)S(1)} fusion(s32[4,32]{1,0:T(4,128)} %param.23, s32[8]{0:T(128)S(1)} %xor_xor_fusion, s32[2]{0:T(128)S(1)} %iota_add_fusion), kind=kLoop, calls=%fused_computation.8 | loop fusion | flops 10224 | bytes 616 | tf_op jit(solution)/shard_map/reduce_sum | solution.py:251
  8.5 0.1 copy.21
  8.5 0.1 eq.65
  8.6 1.6 %collective-permute-done.1 = bf16[4,32,256]{2,1,0:T(8,128)(2,1)S(1)} collective-permute-done((bf16[4,32,256]{2,1,0:T(8,128)(2,1)S(1)}, bf16[4,32,256]{2,1,0:T(8,128)(2,1)S(1)}, u32[]{:S(2)}, u32[]{:S(2)}) %collective-permute-start.1) | collective-permute-done | bytes 65568 | tf_op jit(solution)/shard_map/ppermute | solution.py:236
  10.2 0.1 collective-permute-start.2
  10.3 0.1 broadcast_compare_fusion
  10.4 1.3 %collective-permute-done.2 = bf16[8,32,256]{2,1,0:T(8,128)(2,1)S(1)} collective-permute-done((bf16[8,32,256]{2,1,0:T(8,128)(2,1)S(1)}, bf16[8,32,256]{2,1,0:T(8,128)(2,1)S(1)}, u32[]{:S(2)}, u32[]{:S(2)}) %collective-permute-start.2) | collective-permute-done | bytes 131104 | tf_op jit(solution)/shard_map/ppermute | solution.py:236
  11.7 0.3 select_reduce_fusion
  12.0 1.8 %collective-permute-start.3 = (bf16[4,32,256]{2,1,0:T(8,128)(2,1)S(1)}, bf16[4,32,256]{2,1,0:T(8,128)(2,1)S(1)}, u32[]{:S(2)}, u32[]{:S(2)}) collective-permute-start(bf16[4,32,256]{2,1,0:T(8,128)(2,1)S(1)} %slice.25), channel_id=1, source_target_pairs={{0,16},{2,18},{4,20},{6,22},{8,24},{10,26},{12,28},{14,30},{16,0},... | collective-permute-start | bytes 196616 | tf_op jit(solution)/shard_map/ppermute | solution.py:236
  13.7 2.6 %collective-permute-done.3 = bf16[4,32,256]{2,1,0:T(8,128)(2,1)S(1)} collective-permute-done((bf16[4,32,256]{2,1,0:T(8,128)(2,1)S(1)}, bf16[4,32,256]{2,1,0:T(8,128)(2,1)S(1)}, u32[]{:S(2)}, u32[]{:S(2)}) %collective-permute-start.3) | collective-permute-done | bytes 65568 | tf_op jit(solution)/shard_map/ppermute | solution.py:236
  16.3 3.2 %collective-permute-start.4 = (bf16[2,32,256]{2,1,0:T(8,128)(2,1)S(1)}, bf16[2,32,256]{2,1,0:T(8,128)(2,1)S(1)}, u32[]{:S(2)}, u32[]{:S(2)}) collective-permute-start(bf16[2,32,256]{2,1,0:T(8,128)(2,1)S(1)} %slice.27), channel_id=1, source_target_pairs={{0,48},{2,50},{4,52},{6,54},{8,56},{10,58},{12,60},{14,62},{16,32}... | collective-permute-start | bytes 98312 | tf_op jit(solution)/shard_map/ppermute | solution.py:236
  19.5 2.0 %collective-permute-done.4 = bf16[2,32,256]{2,1,0:T(8,128)(2,1)S(1)} collective-permute-done((bf16[2,32,256]{2,1,0:T(8,128)(2,1)S(1)}, bf16[2,32,256]{2,1,0:T(8,128)(2,1)S(1)}, u32[]{:S(2)}, u32[]{:S(2)}) %collective-permute-start.4) | collective-permute-done | bytes 32800 | tf_op jit(solution)/shard_map/ppermute | solution.py:236
  21.6 2.0 %collective-permute-start.5 = (bf16[2,32,256]{2,1,0:T(8,128)(2,1)S(1)}, bf16[2,32,256]{2,1,0:T(8,128)(2,1)S(1)}, u32[]{:S(2)}, u32[]{:S(2)}) collective-permute-start(bf16[2,32,256]{2,1,0:T(8,128)(2,1)S(1)} %slice_add_fusion.1.here), channel_id=1, source_target_pairs={{0,1},{1,0},{2,3},{3,2},{4,5},{5,4},{6,7},{7,6},{8,9},{9,8},{10,11... | collective-permute-start | bytes 98312 | tf_op jit(solution)/shard_map/ppermute | solution.py:262
  23.6 1.0 %select_reduce_fusion.2 = s32[6]{0:T(128)S(1)} fusion(s32[4]{0:T(128)} %param.20, s32[4]{0:T(128)} %param.19, s32[4,32]{1,0:T(4,128)} %param.22, s32[4,32]{1,0:T(4,128)} %param.21, pred[6]{0:T(512)(128)(4,1)S(1)} %get-tuple-element.13, pred[6]{0:T(512)(128)(4,1)S(1)} %get-tuple-element.14, pred[6]{0:T(512)(128)(4,1)S(1)} %get-tuple-element.15, ...), kind=kLoop, calls=%fused_computation.12 | loop fusion | flops 4602 | bytes 1232 | tf_op jit(solution)/shard_map/reduce_sum | solution.py:224
  24.6 0.9 %collective-permute-done.5.across = bf16[2,32,256]{2,1,0:T(8,128)(2,1)S(1)} collective-permute-done((bf16[2,32,256]{2,1,0:T(8,128)(2,1)S(1)}, bf16[2,32,256]{2,1,0:T(8,128)(2,1)S(1)}, u32[]{:S(2)}, u32[]{:S(2)}) %collective-permute-start.5) | collective-permute-done | bytes 32800 | tf_op jit(solution)/shard_map/ppermute | solution.py:262
  25.5 4.2 %collective-permute-start.6 = (bf16[2,32,256]{2,1,0:T(8,128)(2,1)S(1)}, bf16[2,32,256]{2,1,0:T(8,128)(2,1)S(1)}, u32[]{:S(2)}, u32[]{:S(2)}) collective-permute-start(bf16[2,32,256]{2,1,0:T(8,128)(2,1)S(1)} %pad_maximum_fusion.3), channel_id=1, source_target_pairs={{0,65},{1,64},{64,1},{65,0},{2,67},{3,66},{66,3},{67,2},{4,69},{5,... | collective-permute-start | bytes 98312 | tf_op jit(solution)/shard_map/ppermute | solution.py:264
  29.7 1.9 %collective-permute-done.6.far = bf16[2,32,256]{2,1,0:T(8,128)(2,1)S(1)} collective-permute-done((bf16[2,32,256]{2,1,0:T(8,128)(2,1)S(1)}, bf16[2,32,256]{2,1,0:T(8,128)(2,1)S(1)}, u32[]{:S(2)}, u32[]{:S(2)}) %collective-permute-start.6) | collective-permute-done | bytes 32800 | tf_op jit(solution)/shard_map/ppermute | solution.py:264
  31.6 0.0 copy-done.7
  31.6 0.0 copy-done.6
  31.6 0.0 copy-done.8
  31.6 0.0 copy-done.9
  31.6 0.0 copy-done
  31.6 0.0 copy-done.1
  31.6 0.0 copy-done.2
  31.6 0.0 copy-done.3
  31.7 0.0 copy-done.4
  31.7 0.0 copy-done.5
  31.7 12.3 %shard_map.172 = bf16[2,100,384]{2,1,0:T(8,128)(2,1)S(1)} custom-call(s32[6]{0:T(128)S(1)} %fusion.1.info, bf16[2,32,256]{2,1,0:T(8,128)(2,1)S(1)} %slice_add_fusion.1.here, bf16[2,32,256]{2,1,0:T(8,128)(2,1)S(1)} %collective-permute-done.5.across, bf16[2,32,256]{2,1,0:T(8,128)(2,1)S(1)} %collective-permute-done.6.far, f32[384]{0:T(512)S(1)} %copy-done.1, ...), custom_call_target="tpu_custom_call" | custom-call | flops 6178996224 | bytes 16777216 | tf_op jit(solution)/shard_map/pallas_call | solution.py:184
  43.9 0.8 %copy.22 = bf16[1,1,2,100,384]{4,2,3,1,0:T(2,128)(2,1)} copy(bf16[1,1,2,100,384]{4,3,2,1,0:T(8,128)(2,1)S(1)} %bitcast.2) | data formatting | bytes 307200 | tf_op jit(solution)/shard_map/broadcast_in_dim | solution.py:271
  (17 shorter events, 0.1 us)
Async XLA Ops:
  0.0 31.6 %copy-start.7 = (bf16[400,224]{1,0:T(8,128)(2,1)S(1)}, bf16[400,224]{1,0:T(8,128)(2,1)}, u32[]{:S(2)}) copy-start(bf16[400,224]{1,0:T(8,128)(2,1)} %constant.15.clone.to_one_h) | copy-start | bytes 537604
  0.0 31.6 %copy-start.6 = (bf16[512,144]{1,0:T(8,128)(2,1)S(1)}, bf16[512,144]{1,0:T(8,128)(2,1)}, u32[]{:S(2)}) copy-start(bf16[512,144]{1,0:T(8,128)(2,1)} %constant.16.clone.to_two_h) | copy-start | bytes 442372
  0.0 31.6 %copy-start.8 = (bf16[128,224]{1,0:T(8,128)(2,1)S(1)}, bf16[128,224]{1,0:T(8,128)(2,1)}, u32[]{:S(2)}) copy-start(bf16[128,224]{1,0:T(8,128)(2,1)} %constant.17.clone.to_skip_h) | copy-start | bytes 172036
  0.0 31.6 %copy-start.9 = (bf16[112,128]{1,0:T(8,128)(2,1)S(1)}, bf16[112,128]{1,0:T(8,128)(2,1)}, u32[]{:S(2)}) copy-start(bf16[112,128]{1,0:T(8,128)(2,1)} %constant.18.clone.to_out_h) | copy-start | bytes 86020
  0.0 31.6 %copy-start = (bf16[432,384]{1,0:T(8,128)(2,1)S(1)}, bf16[432,384]{1,0:T(8,128)(2,1)}, u32[]{:S(2)}) copy-start(bf16[432,384]{1,0:T(8,128)(2,1)} %w_in_h.1) | copy-start | bytes 995332
  0.0 31.6 %copy-start.1 = (f32[384]{0:T(512)S(1)}, f32[384]{0:T(512)}, u32[]{:S(2)}) copy-start(f32[384]{0:T(512)} %b_in.1) | copy-start | bytes 4612
  0.0 31.6 %copy-start.2 = (f32[384]{0:T(512)S(1)}, f32[384]{0:T(512)}, u32[]{:S(2)}) copy-start(f32[384]{0:T(512)} %gain_one.1) | copy-start | bytes 4612
  0.0 31.6 %copy-start.3 = (f32[384]{0:T(512)S(1)}, f32[384]{0:T(512)}, u32[]{:S(2)}) copy-start(f32[384]{0:T(512)} %b_one.1) | copy-start | bytes 4612
  0.0 31.6 %copy-start.4 = (f32[384]{0:T(512)S(1)}, f32[384]{0:T(512)}, u32[]{:S(2)}) copy-start(f32[384]{0:T(512)} %gain_two.1) | copy-start | bytes 4612
  0.1 31.6 %copy-start.5 = (f32[384]{0:T(512)S(1)}, f32[384]{0:T(512)}, u32[]{:S(2)}) copy-start(f32[384]{0:T(512)} %b_two.1) | copy-start | bytes 4612
  0.1 4.6 %collective-permute-start = (f32[2,1,2,16,256]{4,3,2,1,0:T(8,128)}, f32[2,1,2,16,256]{4,3,2,1,0:T(8,128)S(1)}, u32[]{:S(2)}, u32[]{:S(2)}) collective-permute-start(f32[2,1,2,16,256]{4,3,2,1,0:T(8,128)} %param.18), channel_id=1, source_target_pairs={{0,4},{2,6},{4,0},{6,2},{8,12},{10,14},{12,8},{14,10},{16,20},{18,... | collective-permute-start | bytes 196616 | tf_op jit(solution)/shard_map/ppermute | solution.py:236
  4.6 5.6 %collective-permute-start.1 = (bf16[4,32,256]{2,1,0:T(8,128)(2,1)S(1)}, bf16[4,32,256]{2,1,0:T(8,128)(2,1)S(1)}, u32[]{:S(2)}, u32[]{:S(2)}) collective-permute-start(bf16[4,32,256]{2,1,0:T(8,128)(2,1)S(1)} %bitcast.3), channel_id=1, source_target_pairs={{0,12},{2,14},{4,8},{6,10},{8,4},{10,6},{12,0},{14,2},{16,28},{18,... | collective-permute-start | bytes 196616 | tf_op jit(solution)/shard_map/ppermute | solution.py:236
  10.2 1.4 %collective-permute-start.2 = (bf16[8,32,256]{2,1,0:T(8,128)(2,1)S(1)}, bf16[8,32,256]{2,1,0:T(8,128)(2,1)S(1)}, u32[]{:S(2)}, u32[]{:S(2)}) collective-permute-start(bf16[8,32,256]{2,1,0:T(8,128)(2,1)S(1)} %pad_maximum_fusion.1), channel_id=1, source_target_pairs={{0,2},{2,0},{4,6},{6,4},{8,10},{10,8},{12,14},{14,12},{16,18},{18,... | collective-permute-start | bytes 393224 | tf_op jit(solution)/shard_map/ppermute | solution.py:236
  12.0 4.3 %collective-permute-start.3 = (bf16[4,32,256]{2,1,0:T(8,128)(2,1)S(1)}, bf16[4,32,256]{2,1,0:T(8,128)(2,1)S(1)}, u32[]{:S(2)}, u32[]{:S(2)}) collective-permute-start(bf16[4,32,256]{2,1,0:T(8,128)(2,1)S(1)} %slice.25), channel_id=1, source_target_pairs={{0,16},{2,18},{4,20},{6,22},{8,24},{10,26},{12,28},{14,30},{16,0},... | collective-permute-start | bytes 196616 | tf_op jit(solution)/shard_map/ppermute | solution.py:236
  16.3 5.2 %collective-permute-start.4 = (bf16[2,32,256]{2,1,0:T(8,128)(2,1)S(1)}, bf16[2,32,256]{2,1,0:T(8,128)(2,1)S(1)}, u32[]{:S(2)}, u32[]{:S(2)}) collective-permute-start(bf16[2,32,256]{2,1,0:T(8,128)(2,1)S(1)} %slice.27), channel_id=1, source_target_pairs={{0,48},{2,50},{4,52},{6,54},{8,56},{10,58},{12,60},{14,62},{16,32}... | collective-permute-start | bytes 98312 | tf_op jit(solution)/shard_map/ppermute | solution.py:236
  21.6 3.9 %collective-permute-start.5 = (bf16[2,32,256]{2,1,0:T(8,128)(2,1)S(1)}, bf16[2,32,256]{2,1,0:T(8,128)(2,1)S(1)}, u32[]{:S(2)}, u32[]{:S(2)}) collective-permute-start(bf16[2,32,256]{2,1,0:T(8,128)(2,1)S(1)} %slice_add_fusion.1.here), channel_id=1, source_target_pairs={{0,1},{1,0},{2,3},{3,2},{4,5},{5,4},{6,7},{7,6},{8,9},{9,8},{10,11... | collective-permute-start | bytes 98312 | tf_op jit(solution)/shard_map/ppermute | solution.py:262
  25.5 6.1 %collective-permute-start.6 = (bf16[2,32,256]{2,1,0:T(8,128)(2,1)S(1)}, bf16[2,32,256]{2,1,0:T(8,128)(2,1)S(1)}, u32[]{:S(2)}, u32[]{:S(2)}) collective-permute-start(bf16[2,32,256]{2,1,0:T(8,128)(2,1)S(1)} %pad_maximum_fusion.3), channel_id=1, source_target_pairs={{0,65},{1,64},{64,1},{65,0},{2,67},{3,66},{66,3},{67,2},{4,69},{5,... | collective-permute-start | bytes 98312 | tf_op jit(solution)/shard_map/ppermute | solution.py:264

commit v5 on v3

--- a/solution.py
+++ b/solution.py
@@ -60,110 +60,141 @@
     info, here, across, far, b_in, gain_one, b_one, gain_two, b_two, w_in_h, to_one_h, to_two_h, to_skip_h, to_out_h, w_one, w_two, out,
     w_in, to_one, to_two, to_skip, to_out, lhs, act_one, act_two, skip, middle, w_one_v, w_two_v, small, sems,
 ):
-    tables = []
-    for n, (src, dst) in enumerate(
-        ((w_in_h, w_in), (to_one_h, to_one), (to_two_h, to_two), (to_skip_h, to_skip), (to_out_h, to_out))
-    ):
-        tables.append(pltpu.make_async_copy(src, dst, small.at[n]))
-        tables[n].start()
-    copies = []
-    for n, (src, dst) in enumerate(((w_one, w_one_v), (w_two, w_two_v))):
-        for step in range(3):
-            tap = 2 - step if n == 0 else step
-            copy = pltpu.make_async_copy(
-                src.at[pl.ds(tap * TAPS, TAPS)], dst.at[pl.ds(tap * TAPS, TAPS)], sems.at[n, tap]
+    first_frame = 2 * info[4]
+
+    @pl.when(first_frame < info[3])
+    def _():
+        tables = []
+        for n, (src, dst) in enumerate(
+            ((w_in_h, w_in), (to_one_h, to_one), (to_two_h, to_two), (to_skip_h, to_skip), (to_out_h, to_out))
+        ):
+            tables.append(pltpu.make_async_copy(src, dst, small.at[n]))
+            tables[n].start()
+        copies = []
+        for n, (src, dst) in enumerate(((w_one, w_one_v), (w_two, w_two_v))):
+            for step in range(3):
+                tap = 2 - step if n == 0 else step
+                copy = pltpu.make_async_copy(
+                    src.at[pl.ds(tap * TAPS, TAPS)], dst.at[pl.ds(tap * TAPS, TAPS)], sems.at[n, tap]
+                )
+                copies.append(copy)
+                if tap:
+                    copy.start()
+                else:
+                    pl.when(info[4] == 1)(copy.start)
+        row0, col0, high, count, section = info[0], info[1], (2 + 2 * info[2]) * TS - 3, info[3], info[4]
+        wide, first = info[5], 2 * section - 2
+        bias_in, gain_1, bias_one, gain_2, bias_two = [
+            v[...].reshape(1, CH) for v in (b_in, gain_one, b_one, gain_two, b_two)
+        ]
+
+        lane = lax.broadcasted_iota(jnp.int32, (SPAN * EXT, EXT * ZC), 1)
+        line = lax.broadcasted_iota(jnp.int32, (SPAN * EXT, EXT * ZC), 0)
+        own = here[0].astype(F32) + far[1].astype(F32)
+        other = (across[0].astype(F32) + far[0].astype(F32)) * section.astype(F32)
+        cells = jnp.concatenate([other, own], axis=0) * inside(
+            row0 - 3 + (line & (EXT - 1)), col0 - 3 + lane // ZC, high, wide
+        )
+        rolled = [
+            cells,
+            pltpu.roll(pltpu.roll(cells, SPAN * EXT - 1, 0), 3 * ZC, 1),
+            pltpu.roll(pltpu.roll(cells, SPAN * EXT - 2, 0), 6 * ZC, 1),
+        ]
+        for x in range(STEM):
+            at = [pltpu.roll(r, (EXT * ZC - ZC * x) % (EXT * ZC), 1) if x else r for r in rolled]
+            packed = jnp.where(lane < 3 * ZC, at[0], jnp.where(lane < 6 * ZC, at[1], at[2]))
+            lhs[:, x] = packed.astype(BF16).reshape(SPAN, EXT, EXT * ZC)
+
+        for table in tables:
+            table.wait()
+        pos = lax.broadcasted_iota(jnp.int32, (STEM_ROWS, 1), 0)
+        mask_one = inside(row0 - 2 + (pos & (EXT - 1)), col0 - 2 + (pos >> 4), high, wide)
+        rows = lhs[...].reshape(SPAN * STEM_ROWS, EXT * ZC)[:, : 9 * ZC]
+        part = [
+            dot(rows[: (2 + dt) * STEM_ROWS], w_in[pl.ds(dt * 9 * ZC, 9 * ZC), :]) for dt in range(3)
+        ]
+        acts, skips = [], []
+        for f in range(SPAN):
+            stem = bias_in
+            for dt in range(3):
+                if f + dt - 2 >= 0:
+                    at = (f + dt - 2) * STEM_ROWS
+                    stem = stem + part[dt][at : at + STEM_ROWS]
+            act = activate(stem, gain_1) * mask_one
+            if f < 2:
+                act = act * (first + f >= 0).astype(F32)
+            else:
+                coarse = stem.astype(BF16)
+                fine = (stem - coarse.astype(F32)).astype(BF16)
+                skips.append(jnp.concatenate([coarse, fine], axis=0))
+            acts.append(act.astype(BF16))
+        moved = dot(to_one[...], jnp.concatenate(acts, axis=1)).astype(BF16)
+        for f in range(SPAN):
+            act_one[f] = moved[:, f * CH : (f + 1) * CH].reshape(5, 5, 16, CH)
+        twice = jnp.concatenate([to_skip[...], to_skip[...]], axis=1)
+        moved = dot(twice, jnp.concatenate(skips, axis=1))
+        for f in range(2):
+            skip[f] = moved[:, f * CH : (f + 1) * CH] + bias_two
+
+        def taps(ref, start, frames, side, rows):
+            return jnp.concatenate(
+                [
+                    ref[start : start + frames, dy : dy + side, dx : dx + side].reshape(frames * rows, CH)
+                    for dy in range(3)
+                    for dx in range(3)
+                ],
+                axis=-1,
             )
-            copy.start()
-            copies.append(copy)
-    row0, col0, high, count, section = info[0], info[1], (2 + 2 * info[2]) * TS - 3, info[3], info[4]
-    wide, first = info[5], 2 * section - 2
-    b_in, gain_one, b_one, gain_two, b_two = [
-        v[...].reshape(1, CH) for v in (b_in, gain_one, b_one, gain_two, b_two)
-    ]
-
-    lane = lax.broadcasted_iota(jnp.int32, (SPAN * EXT, EXT * ZC), 1)
-    line = lax.broadcasted_iota(jnp.int32, (SPAN * EXT, EXT * ZC), 0)
-    own = here[0].astype(F32) + far[1].astype(F32)
-    other = (across[0].astype(F32) + far[0].astype(F32)) * section.astype(F32)
-    cells = jnp.concatenate([other, own], axis=0) * inside(
-        row0 - 3 + (line & (EXT - 1)), col0 - 3 + lane // ZC, high, wide
-    )
-    rolled = [
-        cells,
-        pltpu.roll(pltpu.roll(cells, SPAN * EXT - 1, 0), 3 * ZC, 1),
-        pltpu.roll(pltpu.roll(cells, SPAN * EXT - 2, 0), 6 * ZC, 1),
-    ]
-    for x in range(STEM):
-        at = [pltpu.roll(r, (EXT * ZC - ZC * x) % (EXT * ZC), 1) if x else r for r in rolled]
-        packed = jnp.where(lane < 3 * ZC, at[0], jnp.where(lane < 6 * ZC, at[1], at[2]))
-        lhs[:, x] = packed.astype(BF16).reshape(SPAN, EXT, EXT * ZC)
-
-    for table in tables:
-        table.wait()
-    pos = lax.broadcasted_iota(jnp.int32, (STEM_ROWS, 1), 0)
-    mask_one = inside(row0 - 2 + (pos & (EXT - 1)), col0 - 2 + (pos >> 4), high, wide)
-    for f in range(SPAN):
-        stem = b_in
-        for dt in range(3):
-            if f + dt - 2 >= 0:
-                left = lhs[f + dt - 2].reshape(STEM_ROWS, EXT * ZC)[:, : 9 * ZC]
-                stem = stem + dot(left, w_in[pl.ds(dt * 9 * ZC, 9 * ZC), :])
-        act = activate(stem, gain_one) * mask_one
-        if f < 2:
-            act = act * (first + f >= 0).astype(F32)
-        moved = dot(to_one[...], act.astype(BF16))
-        act_one[f] = moved.astype(BF16).reshape(5, 5, 16, CH)
-        if f >= 2:
-            coarse = stem.astype(BF16)
-            fine = (stem - coarse.astype(F32)).astype(BF16)
-            skip[f - 2] = dot(to_skip[...], coarse) + dot(to_skip[...], fine) + b_two
-
-    for step in range(3):
-        dt = 2 - step
-        copies[step].wait()
-        frames = 2 + dt
-        left = jnp.concatenate(
-            [
-                act_one[0:frames, dy : dy + 3, dx : dx + 3].reshape(frames * MID_ROWS, CH)
-                for dy in range(3)
-                for dx in range(3)
-            ],
-            axis=-1,
-        )
-        part = dot(left, w_one_v[pl.ds(dt * TAPS, TAPS), :])
-        rows = pl.ds((SPAN - frames) * MID_ROWS, frames * MID_ROWS)
-        if step == 0:
-            middle[...] = part
-        else:
-            middle[rows, :] += part
-    spot = lax.broadcasted_iota(jnp.int32, (MID_ROWS, 1), 0)
-    block = spot >> 4
-    block_y = (block >= 3).astype(jnp.int32) + (block >= 6).astype(jnp.int32)
-    mid_y = 3 * ((spot >> 2) & 3) + block_y
-    mid_x = 3 * (spot & 3) + block - 3 * block_y
-    mask_two = inside(row0 - 1 + mid_y, col0 - 1 + mid_x, high, wide)
-    for f in range(SPAN):
-        act = activate(middle[pl.ds(f * MID_ROWS, MID_ROWS), :] + b_one, gain_two) * mask_two
-        if f < 2:
-            act = act * (first + f >= 0).astype(F32)
-        act_two[f] = dot(to_two[...], act.astype(BF16)).astype(BF16).reshape(4, 4, 32, CH)
-
-    total = skip[...].reshape(2 * 128, CH)
-    for dt in range(3):
-        copies[3 + dt].wait()
-        left = jnp.concatenate(
-            [
-                act_two[dt : dt + 2, dy : dy + 2, dx : dx + 2].reshape(2 * 128, CH)
-                for dy in range(3)
-                for dx in range(3)
-            ],
-            axis=-1,
-        )
-        total = total + dot(left, w_two_v[pl.ds(dt * TAPS, TAPS), :])
-    for f in range(2):
-        live = first + 2 + f < count
-        final = jnp.where(live, total[f * 128 : (f + 1) * 128], 0.0).astype(BF16)
-        out[f] = dot(to_out[...], final)[: TS * TS].astype(BF16)
+
+        def add_middle(dt):
+            frames = 2 + dt
+            copies[2 - dt].wait()
+            part = dot(taps(act_one, 0, frames, 3, MID_ROWS), w_one_v[pl.ds(dt * TAPS, TAPS), :])
+            rows = pl.ds((SPAN - frames) * MID_ROWS, frames * MID_ROWS)
+            if dt == 2:
+                middle[rows, :] = part
+            else:
+                middle[rows, :] += part
+
+        add_middle(2)
+        add_middle(1)
+
+        @pl.when(section == 1)
+        def _():
+            add_middle(0)
+
+        spot = lax.broadcasted_iota(jnp.int32, (MID_ROWS, 1), 0)
+        block = spot >> 4
+        block_y = (block >= 3).astype(jnp.int32) + (block >= 6).astype(jnp.int32)
+        mid_y = 3 * ((spot >> 2) & 3) + block_y
+        mid_x = 3 * (spot & 3) + block - 3 * block_y
+        mask_two = inside(row0 - 1 + mid_y, col0 - 1 + mid_x, high, wide)
+        for f in range(SPAN):
+            act = activate(middle[pl.ds(f * MID_ROWS, MID_ROWS), :] + bias_one, gain_2) * mask_two
+            if f < 2:
+                act = act * (first + f >= 0).astype(F32)
+            act_two[f] = dot(to_two[...], act.astype(BF16)).astype(BF16).reshape(4, 4, 32, CH)
+
+        def add_last(dt):
+            copies[3 + dt].wait()
+            part = dot(taps(act_two, dt, 2, 2, 128), w_two_v[pl.ds(dt * TAPS, TAPS), :])
+            skip[...] += part.reshape(2, 128, CH)
+
+        @pl.when(section == 1)
+        def _():
+            add_last(0)
+
+        add_last(1)
+        add_last(2)
+        total = skip[...].reshape(2 * 128, CH)
+        for f in range(2):
+            live = first + 2 + f < count
+            final = jnp.where(live, total[f * 128 : (f + 1) * 128], 0.0).astype(BF16)
+            out[f] = dot(to_out[...], final)[: TS * TS].astype(BF16)
+
+    @pl.when(first_frame >= info[3])
+    def _():
+        out[...] = jnp.zeros_like(out)
 
 
 def decode(info, here, across, far, vectors, w_in, w_one, w_two):
@@ -229,6 +260,7 @@
     live = (tile < tiles // 2).astype(F32)
     first = flip(latent, 2) * live
     have = jnp.concatenate([latent.astype(BF16), first.astype(BF16)]).reshape(4, *unit)
+    have, named_by = after(have, decoder_list)
     have = jnp.concatenate([have, flip(have, 6)])
     have = jnp.concatenate([have, flip(have, 1)])
 
@@ -236,7 +268,7 @@
     step = iota(shape, 0)
     hop = (step >> 2) ^ ((step >> 1) & 1) * 6 ^ (step & 1) * 2
     here = (iota(shape, 2) == 2 * video + iota(shape, 1)) & (iota(shape, 3) == tile ^ hop)
-    names = jnp.sum(jnp.where(here, decoder_list, 0), axis=(2, 3))
+    names = jnp.sum(jnp.where(here, named_by, 0), axis=(2, 3))
 
     shape = (8, 8, 2)
     row = iota(shape, 0)

time: 46 us -> 44.3 us (0.963)
  the two profiles are of different devices: /device:TPU:0 before, /device:TPU:96 now
where the time goes in v5:
time: 44.3 us; the launch traced here: 44.1 us
  waiting for transfers between devices  16.7 us (38%)
  Pallas kernels  12.5 us (28%)
  starting transfers between devices  9.73 us (22%)
  other arithmetic  3.9 us (9%)
  local copies, waits for them, and re-layouts  1.01 us (2%)
    pallas_call x1, Pallas kernels, decode(): pl.pallas_call(decode_kernel, out_shape=jax.ShapeDtypeStruct((2, TS * TS,...  12.5 us
    ppermute x5, starting transfers between devices, local(): lax.ppermute(a, 'tile', [(i, i ^ by) for i in range(tiles)])  9.24 us
    ppermute x5, waiting for transfers between devices, local(): lax.ppermute(a, 'tile', [(i, i ^ by) for i in range(tiles)])  9.11 us
    ppermute x1, waiting for transfers between devices, local(): lax.ppermute(outward, ('video', 'section'), [(z, z ^ 3) for z in range(4)])  5.1 us
    ppermute x1, waiting for transfers between devices, local(): across = lax.ppermute(here, 'section', [(0, 1), (1, 0)])  2.5 us
    reduce_sum x1, other arithmetic, slot_info(): jnp.sum(jnp.where((decoder_list == mine)[None] & (which < 4), table, 0),...  1 us
  transfers between devices with their start and end apart: 7, of which 7 were waited for; matrix products, arithmetic and copies ran while one was open for 8% of the time, Pallas kernels for 0%

profile of v5, /device:TPU:96, one launch (start us, length us, event | category | flops | bytes accessed | tf_op | source)
XLA Modules:
  0.0 44.1 jit_solution(15314728576869241509)
XLA Ops:
  0.0 0.0 copy-start.7
  0.0 0.0 copy-start.6
  0.0 0.0 copy-start.8
  0.0 0.0 copy-start.9
  0.0 0.0 copy-start
  0.0 0.0 copy-start.1
  0.0 0.0 copy-start.2
  0.1 0.0 copy-start.3
  0.1 0.0 copy-start.4
  0.1 0.0 copy-start.5
  0.1 1.6 %collective-permute-start = (f32[2,1,2,16,256]{4,3,2,1,0:T(8,128)}, f32[2,1,2,16,256]{4,3,2,1,0:T(8,128)S(1)}, u32[]{:S(2)}, u32[]{:S(2)}) collective-permute-start(f32[2,1,2,16,256]{4,3,2,1,0:T(8,128)} %param.18), channel_id=1, source_target_pairs={{0,4},{2,6},{4,0},{6,2},{8,12},{10,14},{12,8},{14,10},{16,20},{18,... | collective-permute-start | bytes 196616 | tf_op jit(solution)/shard_map/ppermute | solution.py:256
  1.7 0.9 %convert_element_type.11 = bf16[2,1,2,16,256]{4,3,2,1,0:T(8,128)(2,1)S(1)} convert(f32[2,1,2,16,256]{4,3,2,1,0:T(8,128)} %param.18) | non-fusion elementwise | flops 16384 | bytes 98304 | tf_op jit(solution)/shard_map/convert_element_type | solution.py:262
  2.6 0.7 %broadcast_compare_fusion.1 = pred[4,32]{1,0:T(4,128)(4,1)S(1)} fusion(s32[4,32]{1,0:T(4,128)} %param.23, s32[]{:T(128)S(6)} %add.19), kind=kLoop, calls=%fused_computation.16 | loop fusion | flops 128 | bytes 644 | tf_op jit(solution)/shard_map/eq | solution.py:244
  3.3 1.4 %collective-permute-done = f32[2,1,2,16,256]{4,3,2,1,0:T(8,128)S(1)} collective-permute-done((f32[2,1,2,16,256]{4,3,2,1,0:T(8,128)}, f32[2,1,2,16,256]{4,3,2,1,0:T(8,128)S(1)}, u32[]{:S(2)}, u32[]{:S(2)}) %collective-permute-start) | collective-permute-done | bytes 65568 | tf_op jit(solution)/shard_map/ppermute | solution.py:256
  4.7 2.8 %collective-permute-start.1 = (bf16[4,32,256]{2,1,0:T(8,128)(2,1)S(1)}, bf16[4,32,256]{2,1,0:T(8,128)(2,1)S(1)}, u32[]{:S(2)}, u32[]{:S(2)}) collective-permute-start(bf16[4,32,256]{2,1,0:T(8,128)(2,1)S(1)} %bitcast.3), channel_id=1, source_target_pairs={{0,12},{2,14},{4,8},{6,10},{8,4},{10,6},{12,0},{14,2},{16,28},{18,... | collective-permute-start | bytes 196616 | tf_op jit(solution)/shard_map/ppermute | solution.py:256
  7.5 0.9 %select_reduce_fusion.1 = s32[8,2]{0,1:T(2,128)S(1)} fusion(s32[4,32]{1,0:T(4,128)} %param.23, s32[8]{0:T(128)S(1)} %xor_xor_fusion, s32[2]{0:T(128)S(1)} %iota_add_fusion), kind=kLoop, calls=%fused_computation.8 | loop fusion | flops 10224 | bytes 616 | tf_op jit(solution)/shard_map/reduce_sum | solution.py:271
  8.4 0.1 copy.21
  8.5 0.1 eq.65
  8.5 1.7 %collective-permute-done.1 = bf16[4,32,256]{2,1,0:T(8,128)(2,1)S(1)} collective-permute-done((bf16[4,32,256]{2,1,0:T(8,128)(2,1)S(1)}, bf16[4,32,256]{2,1,0:T(8,128)(2,1)S(1)}, u32[]{:S(2)}, u32[]{:S(2)}) %collective-permute-start.1) | collective-permute-done | bytes 65568 | tf_op jit(solution)/shard_map/ppermute | solution.py:256
  10.2 0.1 collective-permute-start.2
  10.3 0.1 broadcast_compare_fusion
  10.4 1.3 %collective-permute-done.2 = bf16[8,32,256]{2,1,0:T(8,128)(2,1)S(1)} collective-permute-done((bf16[8,32,256]{2,1,0:T(8,128)(2,1)S(1)}, bf16[8,32,256]{2,1,0:T(8,128)(2,1)S(1)}, u32[]{:S(2)}, u32[]{:S(2)}) %collective-permute-start.2) | collective-permute-done | bytes 131104 | tf_op jit(solution)/shard_map/ppermute | solution.py:256
  11.7 0.3 select_reduce_fusion
  12.0 1.7 %collective-permute-start.3 = (bf16[4,32,256]{2,1,0:T(8,128)(2,1)S(1)}, bf16[4,32,256]{2,1,0:T(8,128)(2,1)S(1)}, u32[]{:S(2)}, u32[]{:S(2)}) collective-permute-start(bf16[4,32,256]{2,1,0:T(8,128)(2,1)S(1)} %slice.25), channel_id=1, source_target_pairs={{0,16},{2,18},{4,20},{6,22},{8,24},{10,26},{12,28},{14,30},{16,0},... | collective-permute-start | bytes 196616 | tf_op jit(solution)/shard_map/ppermute | solution.py:256
  13.7 2.7 %collective-permute-done.3 = bf16[4,32,256]{2,1,0:T(8,128)(2,1)S(1)} collective-permute-done((bf16[4,32,256]{2,1,0:T(8,128)(2,1)S(1)}, bf16[4,32,256]{2,1,0:T(8,128)(2,1)S(1)}, u32[]{:S(2)}, u32[]{:S(2)}) %collective-permute-start.3) | collective-permute-done | bytes 65568 | tf_op jit(solution)/shard_map/ppermute | solution.py:256
  16.4 3.1 %collective-permute-start.4 = (bf16[2,32,256]{2,1,0:T(8,128)(2,1)S(1)}, bf16[2,32,256]{2,1,0:T(8,128)(2,1)S(1)}, u32[]{:S(2)}, u32[]{:S(2)}) collective-permute-start(bf16[2,32,256]{2,1,0:T(8,128)(2,1)S(1)} %slice.27), channel_id=1, source_target_pairs={{0,48},{2,50},{4,52},{6,54},{8,56},{10,58},{12,60},{14,62},{16,32}... | collective-permute-start | bytes 98312 | tf_op jit(solution)/shard_map/ppermute | solution.py:256
  19.5 2.1 %collective-permute-done.4 = bf16[2,32,256]{2,1,0:T(8,128)(2,1)S(1)} collective-permute-done((bf16[2,32,256]{2,1,0:T(8,128)(2,1)S(1)}, bf16[2,32,256]{2,1,0:T(8,128)(2,1)S(1)}, u32[]{:S(2)}, u32[]{:S(2)}) %collective-permute-start.4) | collective-permute-done | bytes 32800 | tf_op jit(solution)/shard_map/ppermute | solution.py:256
  21.6 0.4 collective-permute-start.5
  22.0 1.0 %select_reduce_fusion.2 = s32[6]{0:T(128)S(1)} fusion(s32[4]{0:T(128)} %param.20, s32[4]{0:T(128)} %param.19, s32[4,32]{1,0:T(4,128)} %param.22, s32[4,32]{1,0:T(4,128)} %param.21, pred[6]{0:T(512)(128)(4,1)S(1)} %get-tuple-element.13, pred[6]{0:T(512)(128)(4,1)S(1)} %get-tuple-element.14, pred[6]{0:T(512)(128)(4,1)S(1)} %get-tuple-element.15, ...), kind=kLoop, calls=%fused_computation.12 | loop fusion | flops 4602 | bytes 1232 | tf_op jit(solution)/shard_map/reduce_sum | solution.py:244
  23.0 2.5 %collective-permute-done.5.across = bf16[2,32,256]{2,1,0:T(8,128)(2,1)S(1)} collective-permute-done((bf16[2,32,256]{2,1,0:T(8,128)(2,1)S(1)}, bf16[2,32,256]{2,1,0:T(8,128)(2,1)S(1)}, u32[]{:S(2)}, u32[]{:S(2)}) %collective-permute-start.5) | collective-permute-done | bytes 32800 | tf_op jit(solution)/shard_map/ppermute | solution.py:282
  25.5 0.1 collective-permute-start.6
  25.6 5.1 %collective-permute-done.6.far = bf16[2,32,256]{2,1,0:T(8,128)(2,1)S(1)} collective-permute-done((bf16[2,32,256]{2,1,0:T(8,128)(2,1)S(1)}, bf16[2,32,256]{2,1,0:T(8,128)(2,1)S(1)}, u32[]{:S(2)}, u32[]{:S(2)}) %collective-permute-start.6) | collective-permute-done | bytes 32800 | tf_op jit(solution)/shard_map/ppermute | solution.py:284
  30.7 0.0 copy-done.7
  30.7 0.0 copy-done.6
  30.7 0.0 copy-done.8
  30.7 0.0 copy-done.9
  30.7 0.0 copy-done
  30.7 0.0 copy-done.1
  30.7 0.0 copy-done.2
  30.8 0.0 copy-done.3
  30.8 0.0 copy-done.4
  30.8 0.0 copy-done.5
  30.8 12.5 %shard_map.172 = bf16[2,100,384]{2,1,0:T(8,128)(2,1)S(1)} custom-call(s32[6]{0:T(128)S(1)} %fusion.1.info, bf16[2,32,256]{2,1,0:T(8,128)(2,1)S(1)} %slice_add_fusion.1.here, bf16[2,32,256]{2,1,0:T(8,128)(2,1)S(1)} %collective-permute-done.5.across, bf16[2,32,256]{2,1,0:T(8,128)(2,1)S(1)} %collective-permute-done.6.far, f32[384]{0:T(512)S(1)} %copy-done.1, ...), custom_call_target="tpu_custom_call" | custom-call | flops 6178996224 | bytes 16777216 | tf_op jit(solution)/shard_map/pallas_call | solution.py:204
  43.3 0.8 %copy.22 = bf16[1,1,2,100,384]{4,2,3,1,0:T(2,128)(2,1)} copy(bf16[1,1,2,100,384]{4,3,2,1,0:T(8,128)(2,1)S(1)} %bitcast.2) | data formatting | bytes 307200 | tf_op jit(solution)/shard_map/broadcast_in_dim | solution.py:291
  (17 shorter events, 0.1 us)
Async XLA Ops:
  0.0 30.7 %copy-start.7 = (bf16[400,224]{1,0:T(8,128)(2,1)S(1)}, bf16[400,224]{1,0:T(8,128)(2,1)}, u32[]{:S(2)}) copy-start(bf16[400,224]{1,0:T(8,128)(2,1)} %constant.15.clone.to_one_h) | copy-start | bytes 537604
  0.0 30.7 %copy-start.6 = (bf16[512,144]{1,0:T(8,128)(2,1)S(1)}, bf16[512,144]{1,0:T(8,128)(2,1)}, u32[]{:S(2)}) copy-start(bf16[512,144]{1,0:T(8,128)(2,1)} %constant.16.clone.to_two_h) | copy-start | bytes 442372
  0.0 30.7 %copy-start.8 = (bf16[128,224]{1,0:T(8,128)(2,1)S(1)}, bf16[128,224]{1,0:T(8,128)(2,1)}, u32[]{:S(2)}) copy-start(bf16[128,224]{1,0:T(8,128)(2,1)} %constant.17.clone.to_skip_h) | copy-start | bytes 172036
  0.0 30.7 %copy-start.9 = (bf16[112,128]{1,0:T(8,128)(2,1)S(1)}, bf16[112,128]{1,0:T(8,128)(2,1)}, u32[]{:S(2)}) copy-start(bf16[112,128]{1,0:T(8,128)(2,1)} %constant.18.clone.to_out_h) | copy-start | bytes 86020
  0.0 30.7 %copy-start = (bf16[432,384]{1,0:T(8,128)(2,1)S(1)}, bf16[432,384]{1,0:T(8,128)(2,1)}, u32[]{:S(2)}) copy-start(bf16[432,384]{1,0:T(8,128)(2,1)} %w_in_h.1) | copy-start | bytes 995332
  0.0 30.7 %copy-start.1 = (f32[384]{0:T(512)S(1)}, f32[384]{0:T(512)}, u32[]{:S(2)}) copy-start(f32[384]{0:T(512)} %b_in.1) | copy-start | bytes 4612
  0.0 30.7 %copy-start.2 = (f32[384]{0:T(512)S(1)}, f32[384]{0:T(512)}, u32[]{:S(2)}) copy-start(f32[384]{0:T(512)} %gain_one.1) | copy-start | bytes 4612
  0.1 30.7 %copy-start.3 = (f32[384]{0:T(512)S(1)}, f32[384]{0:T(512)}, u32[]{:S(2)}) copy-start(f32[384]{0:T(512)} %b_one.1) | copy-start | bytes 4612
  0.1 30.7 %copy-start.4 = (f32[384]{0:T(512)S(1)}, f32[384]{0:T(512)}, u32[]{:S(2)}) copy-start(f32[384]{0:T(512)} %gain_two.1) | copy-start | bytes 4612
  0.1 30.7 %copy-start.5 = (f32[384]{0:T(512)S(1)}, f32[384]{0:T(512)}, u32[]{:S(2)}) copy-start(f32[384]{0:T(512)} %b_two.1) | copy-start | bytes 4612
  0.1 4.6 %collective-permute-start = (f32[2,1,2,16,256]{4,3,2,1,0:T(8,128)}, f32[2,1,2,16,256]{4,3,2,1,0:T(8,128)S(1)}, u32[]{:S(2)}, u32[]{:S(2)}) collective-permute-start(f32[2,1,2,16,256]{4,3,2,1,0:T(8,128)} %param.18), channel_id=1, source_target_pairs={{0,4},{2,6},{4,0},{6,2},{8,12},{10,14},{12,8},{14,10},{16,20},{18,... | collective-permute-start | bytes 196616 | tf_op jit(solution)/shard_map/ppermute | solution.py:256
  4.7 5.6 %collective-permute-start.1 = (bf16[4,32,256]{2,1,0:T(8,128)(2,1)S(1)}, bf16[4,32,256]{2,1,0:T(8,128)(2,1)S(1)}, u32[]{:S(2)}, u32[]{:S(2)}) collective-permute-start(bf16[4,32,256]{2,1,0:T(8,128)(2,1)S(1)} %bitcast.3), channel_id=1, source_target_pairs={{0,12},{2,14},{4,8},{6,10},{8,4},{10,6},{12,0},{14,2},{16,28},{18,... | collective-permute-start | bytes 196616 | tf_op jit(solution)/shard_map/ppermute | solution.py:256
  10.2 1.4 %collective-permute-start.2 = (bf16[8,32,256]{2,1,0:T(8,128)(2,1)S(1)}, bf16[8,32,256]{2,1,0:T(8,128)(2,1)S(1)}, u32[]{:S(2)}, u32[]{:S(2)}) collective-permute-start(bf16[8,32,256]{2,1,0:T(8,128)(2,1)S(1)} %pad_maximum_fusion.1), channel_id=1, source_target_pairs={{0,2},{2,0},{4,6},{6,4},{8,10},{10,8},{12,14},{14,12},{16,18},{18,... | collective-permute-start | bytes 393224 | tf_op jit(solution)/shard_map/ppermute | solution.py:256
  12.0 4.3 %collective-permute-start.3 = (bf16[4,32,256]{2,1,0:T(8,128)(2,1)S(1)}, bf16[4,32,256]{2,1,0:T(8,128)(2,1)S(1)}, u32[]{:S(2)}, u32[]{:S(2)}) collective-permute-start(bf16[4,32,256]{2,1,0:T(8,128)(2,1)S(1)} %slice.25), channel_id=1, source_target_pairs={{0,16},{2,18},{4,20},{6,22},{8,24},{10,26},{12,28},{14,30},{16,0},... | collective-permute-start | bytes 196616 | tf_op jit(solution)/shard_map/ppermute | solution.py:256
  16.4 5.2 %collective-permute-start.4 = (bf16[2,32,256]{2,1,0:T(8,128)(2,1)S(1)}, bf16[2,32,256]{2,1,0:T(8,128)(2,1)S(1)}, u32[]{:S(2)}, u32[]{:S(2)}) collective-permute-start(bf16[2,32,256]{2,1,0:T(8,128)(2,1)S(1)} %slice.27), channel_id=1, source_target_pairs={{0,48},{2,50},{4,52},{6,54},{8,56},{10,58},{12,60},{14,62},{16,32}... | collective-permute-start | bytes 98312 | tf_op jit(solution)/shard_map/ppermute | solution.py:256
  21.6 3.9 %collective-permute-start.5 = (bf16[2,32,256]{2,1,0:T(8,128)(2,1)S(1)}, bf16[2,32,256]{2,1,0:T(8,128)(2,1)S(1)}, u32[]{:S(2)}, u32[]{:S(2)}) collective-permute-start(bf16[2,32,256]{2,1,0:T(8,128)(2,1)S(1)} %slice_add_fusion.1.here), channel_id=1, source_target_pairs={{0,1},{1,0},{2,3},{3,2},{4,5},{5,4},{6,7},{7,6},{8,9},{9,8},{10,11... | collective-permute-start | bytes 98312 | tf_op jit(solution)/shard_map/ppermute | solution.py:282
  25.5 5.2 %collective-permute-start.6 = (bf16[2,32,256]{2,1,0:T(8,128)(2,1)S(1)}, bf16[2,32,256]{2,1,0:T(8,128)(2,1)S(1)}, u32[]{:S(2)}, u32[]{:S(2)}) collective-permute-start(bf16[2,32,256]{2,1,0:T(8,128)(2,1)S(1)} %pad_maximum_fusion.3), channel_id=1, source_target_pairs={{0,65},{1,64},{64,1},{65,0},{2,67},{3,66},{66,3},{67,2},{4,69},{5,... | collective-permute-start | bytes 98312 | tf_op jit(solution)/shard_map/ppermute | solution.py:284

commit v6 on v5

--- a/solution.py
+++ b/solution.py
@@ -91,7 +91,7 @@
         lane = lax.broadcasted_iota(jnp.int32, (SPAN * EXT, EXT * ZC), 1)
         line = lax.broadcasted_iota(jnp.int32, (SPAN * EXT, EXT * ZC), 0)
         own = here[0].astype(F32) + far[1].astype(F32)
-        other = (across[0].astype(F32) + far[0].astype(F32)) * section.astype(F32)
+        other = (across[...].astype(F32) + far[0].astype(F32)) * section.astype(F32)
         cells = jnp.concatenate([other, own], axis=0) * inside(
             row0 - 3 + (line & (EXT - 1)), col0 - 3 + lane // ZC, high, wide
         )
@@ -258,10 +258,9 @@
     after = lambda done, *args: lax.optimization_barrier((done, *args))
 
     live = (tile < tiles // 2).astype(F32)
-    first = flip(latent, 2) * live
-    have = jnp.concatenate([latent.astype(BF16), first.astype(BF16)]).reshape(4, *unit)
+    got = [flip(latent, by) * live for by in (2, 6, 4)]
+    have = jnp.concatenate([a.astype(BF16) for a in (latent, *got)]).reshape(8, *unit)
     have, named_by = after(have, decoder_list)
-    have = jnp.concatenate([have, flip(have, 6)])
     have = jnp.concatenate([have, flip(have, 1)])
 
     shape = (8, 2) + decoder_list.shape
@@ -277,11 +276,10 @@
     kept = jnp.sum(
         jnp.where(match[:, :, None, None], have[None], jnp.zeros((), BF16)), axis=1, dtype=F32
     ).astype(BF16)
-    kept = kept[:4] + flip(kept[4:], 8)
-    here = kept[:2] + flip(kept[2:], 24)
-    across = lax.ppermute(here, "section", [(0, 1), (1, 0)])
-    outward = jnp.stack([here[1], across[1]])
-    far = lax.ppermute(outward, ("video", "section"), [(z, z ^ 3) for z in range(4)])
+    here = kept[:2] + flip(kept[4:6], 8) + flip(kept[2:4], 24) + flip(kept[6:], 16)
+    around = lambda a, by: lax.ppermute(a, ("video", "section"), [(z, z ^ by) for z in range(4)])
+    far = jnp.stack([around(here[1], 3), around(here[1], 2)])
+    across = around(here[0], 1)
 
     _, resolution, frame_counts = after(kept, resolution, frame_counts)
     info = slot_info(

time: 44.3 us -> 40.8 us (0.921)
  the two profiles are of different devices: /device:TPU:96 before, /device:TPU:0 now
where the time goes in v6:
time: 40.8 us; the launch traced here: 40.5 us
  starting transfers between devices  14.1 us (35%)
  waiting for transfers between devices  11.1 us (27%)
  Pallas kernels  10.2 us (25%)
  other arithmetic  3.94 us (10%)
  local copies, waits for them, and re-layouts  1 us (2%)
    pallas_call x1, Pallas kernels, decode(): pl.pallas_call(decode_kernel, out_shape=jax.ShapeDtypeStruct((2, TS * TS,...  10.2 us
    ppermute x7, starting transfers between devices, local(): lax.ppermute(a, 'tile', [(i, i ^ by) for i in range(tiles)])  8.99 us
    ppermute x7, waiting for transfers between devices, local(): lax.ppermute(a, 'tile', [(i, i ^ by) for i in range(tiles)])  6.77 us
    ppermute x3, starting transfers between devices, local(): lax.ppermute(a, ('video', 'section'), [(z, z ^ by) for z in range(4)])  5.07 us
    ppermute x3, waiting for transfers between devices, local(): lax.ppermute(a, ('video', 'section'), [(z, z ^ by) for z in range(4)])  4.29 us
    reduce_sum x1, other arithmetic, slot_info(): jnp.sum(jnp.where((decoder_list == mine)[None] & (which < 4), table, 0),...  1 us
    convert_element_type x4, other arithmetic, local(): a.astype(BF16)  0.93 us
    reduce_sum x1, other arithmetic, local(): names = jnp.sum(jnp.where(here, named_by, 0), axis=(2, 3))  0.87 us
  transfers between devices with their start and end apart: 10, of which 6 were waited for; matrix products, arithmetic and copies ran while one was open for 9% of the time, Pallas kernels for 0%

profile of v6, /device:TPU:0, one launch (start us, length us, event | category | flops | bytes accessed | tf_op | source)
XLA Modules:
  0.0 40.5 jit_solution(3616255956961080485)
XLA Ops:
  0.0 0.0 copy-start.7
  0.0 0.0 copy-start.6
  0.0 0.0 copy-start.8
  0.0 0.0 copy-start.1
  0.0 0.0 copy-start.2
  0.0 0.0 copy-start.3
  0.0 0.0 copy-start.4
  0.1 0.0 copy-start.5
  0.1 3.2 %collective-permute-start.2 = (f32[2,1,2,16,256]{4,3,2,1,0:T(8,128)}, f32[2,1,2,16,256]{4,3,2,1,0:T(8,128)S(1)}, u32[]{:S(2)}, u32[]{:S(2)}) collective-permute-start(f32[2,1,2,16,256]{4,3,2,1,0:T(8,128)} %param.18), channel_id=1, source_target_pairs={{0,8},{2,10},{4,12},{6,14},{8,0},{10,2},{12,4},{14,6},{16,24},{18,... | collective-permute-start | bytes 196616 | tf_op jit(solution)/shard_map/ppermute | solution.py:256
  3.3 1.1 %collective-permute-start.1 = (f32[2,1,2,16,256]{4,3,2,1,0:T(8,128)}, f32[2,1,2,16,256]{4,3,2,1,0:T(8,128)S(1)}, u32[]{:S(2)}, u32[]{:S(2)}) collective-permute-start(f32[2,1,2,16,256]{4,3,2,1,0:T(8,128)} %param.18), channel_id=1, source_target_pairs={{0,12},{2,14},{4,8},{6,10},{8,4},{10,6},{12,0},{14,2},{16,28},{18,... | collective-permute-start | bytes 196616 | tf_op jit(solution)/shard_map/ppermute | solution.py:256
  4.4 0.0 collective-permute-start
  4.4 0.9 %convert_element_type.17 = bf16[2,1,2,16,256]{4,3,2,1,0:T(8,128)(2,1)S(1)} convert(f32[2,1,2,16,256]{4,3,2,1,0:T(8,128)} %param.18) | non-fusion elementwise | flops 16384 | bytes 98304 | tf_op jit(solution)/shard_map/convert_element_type | solution.py:262
  5.4 0.7 %broadcast_compare_fusion.1 = pred[4,32]{1,0:T(4,128)(4,1)S(1)} fusion(s32[4,32]{1,0:T(4,128)} %param.23, s32[]{:T(128)S(6)} %add.22), kind=kLoop, calls=%fused_computation.20 | loop fusion | flops 128 | bytes 644 | tf_op jit(solution)/shard_map/eq | solution.py:244
  6.1 0.0 collective-permute-done.2
  6.1 2.8 %collective-permute-done.1 = f32[2,1,2,16,256]{4,3,2,1,0:T(8,128)S(1)} collective-permute-done((f32[2,1,2,16,256]{4,3,2,1,0:T(8,128)}, f32[2,1,2,16,256]{4,3,2,1,0:T(8,128)S(1)}, u32[]{:S(2)}, u32[]{:S(2)}) %collective-permute-start.1) | collective-permute-done | bytes 65568 | tf_op jit(solution)/shard_map/ppermute | solution.py:256
  9.0 0.0 collective-permute-done
  9.0 0.1 collective-permute-start.3
  9.1 0.9 %select_reduce_fusion.1 = s32[8,2]{0,1:T(2,128)S(1)} fusion(s32[4,32]{1,0:T(4,128)} %param.23, s32[8]{0:T(128)S(1)} %xor_xor_fusion, s32[2]{0:T(128)S(1)} %iota_add_fusion), kind=kLoop, calls=%fused_computation.10 | loop fusion | flops 10224 | bytes 616 | tf_op jit(solution)/shard_map/reduce_sum | solution.py:270
  10.0 0.1 copy.21
  10.1 0.1 eq.65
  10.2 0.1 broadcast_compare_fusion
  10.2 0.2 collective-permute-done.3
  10.5 0.3 select_reduce_fusion
  10.8 1.7 %collective-permute-start.4 = (bf16[2,32,256]{2,1,0:T(8,128)(2,1)S(1)}, bf16[2,32,256]{2,1,0:T(8,128)(2,1)S(1)}, u32[]{:S(2)}, u32[]{:S(2)}) collective-permute-start(bf16[2,32,256]{2,1,0:T(8,128)(2,1)S(1)} %get-tuple-element.13), channel_id=1, source_target_pairs={{0,16},{2,18},{4,20},{6,22},{8,24},{10,26},{12,28},{14,30},{16,0},... | collective-permute-start | bytes 98312 | tf_op jit(solution)/shard_map/ppermute | solution.py:256
  12.4 2.2 %collective-permute-start.5 = (bf16[2,32,256]{2,1,0:T(8,128)(2,1)S(1)}, bf16[2,32,256]{2,1,0:T(8,128)(2,1)S(1)}, u32[]{:S(2)}, u32[]{:S(2)}) collective-permute-start(bf16[2,32,256]{2,1,0:T(8,128)(2,1)S(1)} %get-tuple-element.15), channel_id=1, source_target_pairs={{0,48},{2,50},{4,52},{6,54},{8,56},{10,58},{12,60},{14,62},{16,32}... | collective-permute-start | bytes 98312 | tf_op jit(solution)/shard_map/ppermute | solution.py:256
  14.6 0.7 %collective-permute-start.6 = (bf16[2,32,256]{2,1,0:T(8,128)(2,1)S(1)}, bf16[2,32,256]{2,1,0:T(8,128)(2,1)S(1)}, u32[]{:S(2)}, u32[]{:S(2)}) collective-permute-start(bf16[2,32,256]{2,1,0:T(8,128)(2,1)S(1)} %get-tuple-element.14), channel_id=1, source_target_pairs={{0,32},{2,34},{4,36},{6,38},{8,40},{10,42},{12,44},{14,46},{16,48}... | collective-permute-start | bytes 98312 | tf_op jit(solution)/shard_map/ppermute | solution.py:256
  15.3 1.0 %select_reduce_fusion.2 = s32[6]{0:T(128)S(1)} fusion(s32[4]{0:T(128)} %param.20, s32[4]{0:T(128)} %param.19, s32[4,32]{1,0:T(4,128)} %param.22, s32[4,32]{1,0:T(4,128)} %param.21, pred[6]{0:T(512)(128)(4,1)S(1)} %get-tuple-element.18, pred[6]{0:T(512)(128)(4,1)S(1)} %get-tuple-element.19, pred[6]{0:T(512)(128)(4,1)S(1)} %get-tuple-element.20, ...), kind=kLoop, calls=%fused_computation.16 | loop fusion | flops 4602 | bytes 1232 | tf_op jit(solution)/shard_map/reduce_sum | solution.py:244
  16.3 0.0 collective-permute-done.4
  16.4 1.2 %collective-permute-done.5 = bf16[2,32,256]{2,1,0:T(8,128)(2,1)S(1)} collective-permute-done((bf16[2,32,256]{2,1,0:T(8,128)(2,1)S(1)}, bf16[2,32,256]{2,1,0:T(8,128)(2,1)S(1)}, u32[]{:S(2)}, u32[]{:S(2)}) %collective-permute-start.5) | collective-permute-done | bytes 32800 | tf_op jit(solution)/shard_map/ppermute | solution.py:256
  17.6 2.5 %collective-permute-done.6 = bf16[2,32,256]{2,1,0:T(8,128)(2,1)S(1)} collective-permute-done((bf16[2,32,256]{2,1,0:T(8,128)(2,1)S(1)}, bf16[2,32,256]{2,1,0:T(8,128)(2,1)S(1)}, u32[]{:S(2)}, u32[]{:S(2)}) %collective-permute-start.6) | collective-permute-done | bytes 32800 | tf_op jit(solution)/shard_map/ppermute | solution.py:256
  20.1 4.1 %collective-permute-start.8 = (bf16[32,256]{1,0:T(8,128)(2,1)S(1)}, bf16[32,256]{1,0:T(8,128)(2,1)S(1)}, u32[]{:S(2)}, u32[]{:S(2)}) collective-permute-start(bf16[32,256]{1,0:T(8,128)(2,1)S(1)} %get-tuple-element.16), channel_id=1, source_target_pairs={{0,65},{1,64},{64,1},{65,0},{2,67},{3,66},{66,3},{67,2},{4,69},{5,... | collective-permute-start | bytes 49160 | tf_op jit(solution)/shard_map/ppermute | solution.py:280
  24.2 0.0 collective-permute-start.9
  24.2 0.9 %collective-permute-start.7 = (bf16[32,256]{1,0:T(8,128)(2,1)S(1)}, bf16[32,256]{1,0:T(8,128)(2,1)S(1)}, u32[]{:S(2)}, u32[]{:S(2)}) collective-permute-start(bf16[32,256]{1,0:T(8,128)(2,1)S(1)} %get-tuple-element.17), channel_id=1, source_target_pairs={{0,1},{1,0},{64,65},{65,64},{2,3},{3,2},{66,67},{67,66},{4,5},{5,4... | collective-permute-start | bytes 49160 | tf_op jit(solution)/shard_map/ppermute | solution.py:280
  25.1 0.8 %collective-permute-done.8 = bf16[32,256]{1,0:T(8,128)(2,1)S(1)} collective-permute-done((bf16[32,256]{1,0:T(8,128)(2,1)S(1)}, bf16[32,256]{1,0:T(8,128)(2,1)S(1)}, u32[]{:S(2)}, u32[]{:S(2)}) %collective-permute-start.8) | collective-permute-done | bytes 16416 | tf_op jit(solution)/shard_map/ppermute | solution.py:280
  25.9 3.5 %collective-permute-done.9 = bf16[32,256]{1,0:T(8,128)(2,1)S(1)} collective-permute-done((bf16[32,256]{1,0:T(8,128)(2,1)S(1)}, bf16[32,256]{1,0:T(8,128)(2,1)S(1)}, u32[]{:S(2)}, u32[]{:S(2)}) %collective-permute-start.9) | collective-permute-done | bytes 16416 | tf_op jit(solution)/shard_map/ppermute | solution.py:280
  29.4 0.0 collective-permute-done.7.across
  29.4 0.0 copy-done.7
  29.4 0.0 copy-done.6
  29.5 0.0 copy-done.8
  29.5 0.0 copy-done.9
  29.5 0.0 copy-done
  29.5 0.0 copy-done.1
  29.5 0.0 copy-done.2
  29.5 0.0 copy-done.3
  29.5 0.0 copy-done.4
  29.5 0.0 copy-done.5
  29.5 10.2 %shard_map.172 = bf16[2,100,384]{2,1,0:T(8,128)(2,1)S(1)} custom-call(s32[6]{0:T(128)S(1)} %fusion.3.info, bf16[2,32,256]{2,1,0:T(8,128)(2,1)S(1)} %fusion.1.here, bf16[32,256]{1,0:T(8,128)(2,1)S(1)} %collective-permute-done.7.across, bf16[2,32,256]{2,1,0:T(8,128)(2,1)S(1)} %pad_maximum_fusion.2.far, f32[384]{0:T(512)S(1)} %copy-done.1, f32[384]{0:T(512)S(1)} %copy-done.2, ...), custom_call_target="tpu_custom_call" | custom-call | flops 6178996224 | bytes 16777216 | tf_op jit(solution)/shard_map/pallas_call | solution.py:204
  39.7 0.8 %copy.22 = bf16[1,1,2,100,384]{4,2,3,1,0:T(2,128)(2,1)} copy(bf16[1,1,2,100,384]{4,3,2,1,0:T(8,128)(2,1)S(1)} %bitcast.8) | data formatting | bytes 307200 | tf_op jit(solution)/shard_map/broadcast_in_dim | solution.py:289
  (17 shorter events, 0.1 us)
Async XLA Ops:
  0.0 29.4 %copy-start.7 = (bf16[400,224]{1,0:T(8,128)(2,1)S(1)}, bf16[400,224]{1,0:T(8,128)(2,1)}, u32[]{:S(2)}) copy-start(bf16[400,224]{1,0:T(8,128)(2,1)} %constant.15.clone.to_one_h) | copy-start | bytes 537604
  0.0 29.4 %copy-start.6 = (bf16[512,144]{1,0:T(8,128)(2,1)S(1)}, bf16[512,144]{1,0:T(8,128)(2,1)}, u32[]{:S(2)}) copy-start(bf16[512,144]{1,0:T(8,128)(2,1)} %constant.16.clone.to_two_h) | copy-start | bytes 442372
  0.0 29.4 %copy-start.8 = (bf16[128,224]{1,0:T(8,128)(2,1)S(1)}, bf16[128,224]{1,0:T(8,128)(2,1)}, u32[]{:S(2)}) copy-start(bf16[128,224]{1,0:T(8,128)(2,1)} %constant.17.clone.to_skip_h) | copy-start | bytes 172036
  0.0 29.5 %copy-start.9 = (bf16[112,128]{1,0:T(8,128)(2,1)S(1)}, bf16[112,128]{1,0:T(8,128)(2,1)}, u32[]{:S(2)}) copy-start(bf16[112,128]{1,0:T(8,128)(2,1)} %constant.18.clone.to_out_h) | copy-start | bytes 86020
  0.0 29.5 %copy-start = (bf16[432,384]{1,0:T(8,128)(2,1)S(1)}, bf16[432,384]{1,0:T(8,128)(2,1)}, u32[]{:S(2)}) copy-start(bf16[432,384]{1,0:T(8,128)(2,1)} %w_in_h.1) | copy-start | bytes 995332
  0.0 29.5 %copy-start.1 = (f32[384]{0:T(512)S(1)}, f32[384]{0:T(512)}, u32[]{:S(2)}) copy-start(f32[384]{0:T(512)} %b_in.1) | copy-start | bytes 4612
  0.0 29.5 %copy-start.2 = (f32[384]{0:T(512)S(1)}, f32[384]{0:T(512)}, u32[]{:S(2)}) copy-start(f32[384]{0:T(512)} %gain_one.1) | copy-start | bytes 4612
  0.0 29.5 %copy-start.3 = (f32[384]{0:T(512)S(1)}, f32[384]{0:T(512)}, u32[]{:S(2)}) copy-start(f32[384]{0:T(512)} %b_one.1) | copy-start | bytes 4612
  0.0 29.5 %copy-start.4 = (f32[384]{0:T(512)S(1)}, f32[384]{0:T(512)}, u32[]{:S(2)}) copy-start(f32[384]{0:T(512)} %gain_two.1) | copy-start | bytes 4612
  0.1 29.5 %copy-start.5 = (f32[384]{0:T(512)S(1)}, f32[384]{0:T(512)}, u32[]{:S(2)}) copy-start(f32[384]{0:T(512)} %b_two.1) | copy-start | bytes 4612
  0.1 6.1 %collective-permute-start.2 = (f32[2,1,2,16,256]{4,3,2,1,0:T(8,128)}, f32[2,1,2,16,256]{4,3,2,1,0:T(8,128)S(1)}, u32[]{:S(2)}, u32[]{:S(2)}) collective-permute-start(f32[2,1,2,16,256]{4,3,2,1,0:T(8,128)} %param.18), channel_id=1, source_target_pairs={{0,8},{2,10},{4,12},{6,14},{8,0},{10,2},{12,4},{14,6},{16,24},{18,... | collective-permute-start | bytes 196616 | tf_op jit(solution)/shard_map/ppermute | solution.py:256
  3.3 5.7 %collective-permute-start.1 = (f32[2,1,2,16,256]{4,3,2,1,0:T(8,128)}, f32[2,1,2,16,256]{4,3,2,1,0:T(8,128)S(1)}, u32[]{:S(2)}, u32[]{:S(2)}) collective-permute-start(f32[2,1,2,16,256]{4,3,2,1,0:T(8,128)} %param.18), channel_id=1, source_target_pairs={{0,12},{2,14},{4,8},{6,10},{8,4},{10,6},{12,0},{14,2},{16,28},{18,... | collective-permute-start | bytes 196616 | tf_op jit(solution)/shard_map/ppermute | solution.py:256
  4.4 4.6 %collective-permute-start = (f32[2,1,2,16,256]{4,3,2,1,0:T(8,128)}, f32[2,1,2,16,256]{4,3,2,1,0:T(8,128)S(1)}, u32[]{:S(2)}, u32[]{:S(2)}) collective-permute-start(f32[2,1,2,16,256]{4,3,2,1,0:T(8,128)} %param.18), channel_id=1, source_target_pairs={{0,4},{2,6},{4,0},{6,2},{8,12},{10,14},{12,8},{14,10},{16,20},{18,... | collective-permute-start | bytes 196616 | tf_op jit(solution)/shard_map/ppermute | solution.py:256
  9.0 1.4 %collective-permute-start.3 = (bf16[8,32,256]{2,1,0:T(8,128)(2,1)S(1)}, bf16[8,32,256]{2,1,0:T(8,128)(2,1)S(1)}, u32[]{:S(2)}, u32[]{:S(2)}) collective-permute-start(bf16[8,32,256]{2,1,0:T(8,128)(2,1)S(1)} %bitcast.9), channel_id=1, source_target_pairs={{0,2},{2,0},{4,6},{6,4},{8,10},{10,8},{12,14},{14,12},{16,18},{18,... | collective-permute-start | bytes 393224 | tf_op jit(solution)/shard_map/ppermute | solution.py:256
  10.8 5.6 %collective-permute-start.4 = (bf16[2,32,256]{2,1,0:T(8,128)(2,1)S(1)}, bf16[2,32,256]{2,1,0:T(8,128)(2,1)S(1)}, u32[]{:S(2)}, u32[]{:S(2)}) collective-permute-start(bf16[2,32,256]{2,1,0:T(8,128)(2,1)S(1)} %get-tuple-element.13), channel_id=1, source_target_pairs={{0,16},{2,18},{4,20},{6,22},{8,24},{10,26},{12,28},{14,30},{16,0},... | collective-permute-start | bytes 98312 | tf_op jit(solution)/shard_map/ppermute | solution.py:256
  12.4 5.1 %collective-permute-start.5 = (bf16[2,32,256]{2,1,0:T(8,128)(2,1)S(1)}, bf16[2,32,256]{2,1,0:T(8,128)(2,1)S(1)}, u32[]{:S(2)}, u32[]{:S(2)}) collective-permute-start(bf16[2,32,256]{2,1,0:T(8,128)(2,1)S(1)} %get-tuple-element.15), channel_id=1, source_target_pairs={{0,48},{2,50},{4,52},{6,54},{8,56},{10,58},{12,60},{14,62},{16,32}... | collective-permute-start | bytes 98312 | tf_op jit(solution)/shard_map/ppermute | solution.py:256
  14.6 5.4 %collective-permute-start.6 = (bf16[2,32,256]{2,1,0:T(8,128)(2,1)S(1)}, bf16[2,32,256]{2,1,0:T(8,128)(2,1)S(1)}, u32[]{:S(2)}, u32[]{:S(2)}) collective-permute-start(bf16[2,32,256]{2,1,0:T(8,128)(2,1)S(1)} %get-tuple-element.14), channel_id=1, source_target_pairs={{0,32},{2,34},{4,36},{6,38},{8,40},{10,42},{12,44},{14,46},{16,48}... | collective-permute-start | bytes 98312 | tf_op jit(solution)/shard_map/ppermute | solution.py:256
  20.1 5.8 %collective-permute-start.8 = (bf16[32,256]{1,0:T(8,128)(2,1)S(1)}, bf16[32,256]{1,0:T(8,128)(2,1)S(1)}, u32[]{:S(2)}, u32[]{:S(2)}) collective-permute-start(bf16[32,256]{1,0:T(8,128)(2,1)S(1)} %get-tuple-element.16), channel_id=1, source_target_pairs={{0,65},{1,64},{64,1},{65,0},{2,67},{3,66},{66,3},{67,2},{4,69},{5,... | collective-permute-start | bytes 49160 | tf_op jit(solution)/shard_map/ppermute | solution.py:280
  24.2 5.2 %collective-permute-start.9 = (bf16[32,256]{1,0:T(8,128)(2,1)S(1)}, bf16[32,256]{1,0:T(8,128)(2,1)S(1)}, u32[]{:S(2)}, u32[]{:S(2)}) collective-permute-start(bf16[32,256]{1,0:T(8,128)(2,1)S(1)} %get-tuple-element.16), channel_id=1, source_target_pairs={{0,64},{1,65},{64,0},{65,1},{2,66},{3,67},{66,2},{67,3},{4,68},{5,... | collective-permute-start | bytes 49160 | tf_op jit(solution)/shard_map/ppermute | solution.py:280
  24.2 5.2 %collective-permute-start.7 = (bf16[32,256]{1,0:T(8,128)(2,1)S(1)}, bf16[32,256]{1,0:T(8,128)(2,1)S(1)}, u32[]{:S(2)}, u32[]{:S(2)}) collective-permute-start(bf16[32,256]{1,0:T(8,128)(2,1)S(1)} %get-tuple-element.17), channel_id=1, source_target_pairs={{0,1},{1,0},{64,65},{65,64},{2,3},{3,2},{66,67},{67,66},{4,5},{5,4... | collective-permute-start | bytes 49160 | tf_op jit(solution)/shard_map/ppermute | solution.py:280
